TPU v7x, 128 devices: a whole 4x4x4 slice. The times are simulated.
128 devices in a mesh: gx: 4 (over z_hi, core), gy: 4 (over x), gz: 8 (over y, z_lo).
Axes of the slice: x: 4, y: 4, z: 4 (z_hi: 2, z_lo: 2; z = z_hi * 2 + z_lo), core: 2. Of those that a mesh axis runs over, the one named last changes fastest.
Arguments:
- offsets: float32 [16, 16, 16, 3, 16], P('gx', 'gy', 'gz'), as said below
- species: int32 [16, 16, 16, 16], P('gx', 'gy', 'gz'), may hold values from 0 to 3
- neighbours: int32 [16, 16, 16, 16, 32], P('gx', 'gy', 'gz'), may hold values from 0 to 6143
- counts: int32 [16, 16, 16, 16], P('gx', 'gy', 'gz'), may hold values from 8 to 32, as said below
- embed: float32 [4, 128], replicated, may hold values from 0.25 to 1.75
- radial_a: float32 [8, 128], replicated, may hold values from -2 to 2
- mix_in: bfloat16 [384, 128], replicated, may hold values from -0.3125 to 0.3125
- proj_center: bfloat16 [128, 128], replicated, may hold values from -0.5 to 0.5
- proj_neigh: bfloat16 [128, 128], replicated, may hold values from -0.5 to 0.5
- radial_b: float32 [8, 128], replicated, may hold values from -2 to 2
- couple: float32 [3, 128], replicated, may hold values from -4 to 4
- latent_two: bfloat16 [128, 128], replicated, may hold values from -0.5 to 0.5
- latent_three: bfloat16 [128, 128], replicated, may hold values from -0.5 to 0.5
- readout: float32 [128], replicated, may hold values from -0.5 to 0.5
Outputs:
- forces: float32 [16, 16, 16, 3, 16], P('gx', 'gy', 'gz')
- atom_energy: float32 [16, 16, 16, 16], P('gx', 'gy', 'gz')
Inputs may be any that keep to these rules, and one draw needn't show every extreme that they name: Slots 0 to count - 1 of an atom are live; the level of the counts differs from brick to brick, and the first atom of each brick has all 32. `offsets`: each atom lies within 0.1 of its own site in its cell: x at 0.5 + (slot % 2), y at 0.5 + (slot // 2 % 2), z at (slot // 4 + 0.5) * 8 / 16.
All inputs are finite; a program needn't handle non-finite values.
Results may differ from a plain program's by a relative error of at most 0.014.
Values may be sent and summed in bfloat16 or wider, within the bound.
No kernel may reach another device: no remote copies, remote signals or barrier semaphores. Data moves between devices by JAX's collectives and lax.ppermute only.
A program may use at most 128 MiB of HBM per device.

v0:
```python
import math

import jax
import jax.numpy as jnp
from jax import lax
from jax.sharding import PartitionSpec as P

CX = 4
CY = 4
CZ = 2
PER_CELL = 16
SLOTS = 32
CH = 128
NBASIS = 8
SPECIES = 4


CELL_SIDE = 2.0
CUTOFF = 10.5
NORM_EPS = 1e-05


def passed_along(block, axis, distance):
    devices = range(lax.axis_size(axis))
    route = [((i - distance) % len(devices), i) for i in devices]
    return lax.ppermute(block, axis, route)


def padded(array, sides, width):
    for axis, dim in sides:
        size, length = (lax.axis_size(axis), array.shape[dim])
        up = [(i, (i + 1) % size) for i in range(size)]
        down = [(j, i) for i, j in up]
        last = lax.slice_in_dim(array, length - width, length, axis=dim)
        first = lax.slice_in_dim(array, 0, width, axis=dim)
        before = lax.ppermute(last, axis, up)
        after = lax.ppermute(first, axis, down)
        array = jnp.concatenate([before, array, after], axis=dim)
    return array


def harmonics(unit_x, unit_y, unit_z):
    root_three = math.sqrt(3.0)
    root_five = math.sqrt(5.0)
    root_fifteen = math.sqrt(15.0)
    return jnp.stack(
        [
            jnp.ones_like(unit_x),
            root_three * unit_x,
            root_three * unit_y,
            root_three * unit_z,
            root_fifteen * unit_x * unit_y,
            root_fifteen * unit_y * unit_z,
            0.5 * root_five * (3.0 * unit_z * unit_z - 1.0),
            root_fifteen * unit_x * unit_z,
            0.5 * root_fifteen * (unit_x * unit_x - unit_y * unit_y),
        ],
        0,
    )


def layer_geometry(flat_offsets, layer_nbr, layer_count, layer_index):
    ext_y = CY + 4
    ext_z = CZ + 4
    layer_rows = CY * CZ * PER_CELL
    atom_index = jnp.arange(layer_rows, dtype=jnp.int32)
    atom_slot = atom_index % PER_CELL
    cell_z = atom_index // PER_CELL % CZ
    cell_y = atom_index // (PER_CELL * CZ)
    self_ext = (
        ((layer_index + 2) * ext_y + cell_y + 2) * ext_z + cell_z + 2
    ) * PER_CELL + atom_slot
    own_place = flat_offsets[self_ext]
    other_place = flat_offsets[layer_nbr]
    other_cell = layer_nbr // PER_CELL
    shift_z = other_cell % ext_z - 2 - cell_z[:, None]
    shift_y = other_cell // ext_z % ext_y - 2 - cell_y[:, None]
    shift_x = other_cell // (ext_z * ext_y) - 2 - layer_index
    step_x = shift_x.astype(jnp.float32) * CELL_SIDE + other_place[:, :, 0] - own_place[:, None, 0]
    step_y = shift_y.astype(jnp.float32) * CELL_SIDE + other_place[:, :, 1] - own_place[:, None, 1]
    step_z = shift_z.astype(jnp.float32) * CELL_SIDE + other_place[:, :, 2] - own_place[:, None, 2]
    live_mask = (jnp.arange(SLOTS, dtype=jnp.int32)[None, :] < layer_count[:, None]).astype(
        jnp.float32
    )
    return (step_x, step_y, step_z, live_mask)


def pair_basis(step_x, step_y, step_z):
    distance = jnp.sqrt(step_x * step_x + step_y * step_y + step_z * step_z)
    harmonic_values = harmonics(step_x / distance, step_y / distance, step_z / distance)
    orders = jnp.arange(1, NBASIS + 1, dtype=jnp.int32).astype(jnp.float32)
    bessel = (
        CELL_SIDE * jnp.sin(math.pi / CUTOFF * distance[:, :, None] * orders) / distance[:, :, None]
    )
    scaled = distance / CUTOFF
    envelope = (1.0 - scaled * scaled) * (1.0 - scaled * scaled)
    return (harmonic_values, bessel, envelope)


def layer_environment(
    flat_offsets, layer_nbr, layer_count, layer_species, layer_index, embed, radial_a, mix_in
):
    step_x, step_y, step_z, live_mask = layer_geometry(
        flat_offsets, layer_nbr, layer_count, layer_index
    )
    harmonic_values, bessel, envelope = pair_basis(step_x, step_y, step_z)
    radial = jnp.einsum("akn,nc->akc", bessel, radial_a, precision=lax.Precision.HIGHEST)
    weighted = (live_mask * envelope)[:, :, None] * radial
    species_hot = (layer_species[:, None] == jnp.arange(SPECIES, dtype=jnp.int32)[None, :]).astype(
        jnp.float32
    )
    scaling = jnp.dot(species_hot, embed, precision=lax.Precision.HIGHEST) / math.sqrt(SLOTS)
    environment = (
        jnp.einsum("mak,akc->mac", harmonic_values, weighted, precision=lax.Precision.HIGHEST)
        * scaling[None]
    )
    squares = environment * environment
    invariant = jnp.concatenate(
        [squares[0], jnp.sum(squares[1:4], 0), jnp.sum(squares[4:9], 0)], -1
    )
    normed = invariant * lax.rsqrt(jnp.mean(invariant * invariant, -1, keepdims=True) + NORM_EPS)
    hidden_full = jax.nn.silu(
        jnp.dot(normed.astype(jnp.bfloat16), mix_in, preferred_element_type=jnp.float32)
    )
    return (hidden_full, environment)


def layer_energy(
    flat_offsets,
    layer_nbr,
    layer_count,
    layer_index,
    center_rows,
    neigh_rows,
    environment,
    couple,
    radial_b,
    latent_two,
    latent_three,
    readout,
):
    step_x, step_y, step_z, live_mask = layer_geometry(
        flat_offsets, layer_nbr, layer_count, layer_index
    )
    harmonic_values, bessel, envelope = pair_basis(step_x, step_y, step_z)
    gathered = neigh_rows[layer_nbr]
    couple_full = jnp.concatenate(
        [couple[0:1], jnp.repeat(couple[1:2], 3, 0), jnp.repeat(couple[2:3], 5, 0)], 0
    )
    coupled = jnp.einsum(
        "mak,mac->akc",
        harmonic_values,
        environment * couple_full[:, None, :],
        precision=lax.Precision.HIGHEST,
    )
    radial = jnp.einsum("akn,nc->akc", bessel, radial_b, precision=lax.Precision.HIGHEST)
    hidden_one = jax.nn.silu(center_rows[:, None, :] + gathered + coupled + radial).astype(
        jnp.bfloat16
    )
    hidden_one = hidden_one.reshape(-1, CH)
    hidden_two = jax.nn.silu(
        jnp.dot(hidden_one, latent_two, preferred_element_type=jnp.float32)
    ).astype(jnp.bfloat16)
    hidden_three = jax.nn.silu(
        jnp.dot(hidden_two, latent_three, preferred_element_type=jnp.float32)
    )
    pair_out = jnp.dot(hidden_three, readout, precision=lax.Precision.HIGHEST).reshape(
        live_mask.shape
    )
    return jnp.sum(live_mask * envelope * pair_out, -1)


def brick_environment(
    ext_offsets, nbr_layers, count_layers, species_layers, embed, radial_a, mix_in
):
    flat_offsets = jnp.moveaxis(ext_offsets, 3, 4).reshape(-1, 3)

    def one_layer(layer_items):
        layer_index, layer_nbr, layer_count, layer_species = layer_items
        return layer_environment(
            flat_offsets,
            layer_nbr,
            layer_count,
            layer_species,
            layer_index,
            embed,
            radial_a,
            mix_in,
        )

    return lax.map(
        jax.checkpoint(one_layer),
        (jnp.arange(CX, dtype=jnp.int32), nbr_layers, count_layers, species_layers),
    )


def brick_energy(
    ext_offsets,
    center,
    neigh_rows,
    environment,
    nbr_layers,
    count_layers,
    couple,
    radial_b,
    latent_two,
    latent_three,
    readout,
):
    flat_offsets = jnp.moveaxis(ext_offsets, 3, 4).reshape(-1, 3)

    def one_layer(layer_items):
        layer_index, layer_nbr, layer_count, center_rows, layer_env = layer_items
        return layer_energy(
            flat_offsets,
            layer_nbr,
            layer_count,
            layer_index,
            center_rows,
            neigh_rows,
            layer_env,
            couple,
            radial_b,
            latent_two,
            latent_three,
            readout,
        )

    return lax.map(
        jax.checkpoint(one_layer),
        (jnp.arange(CX, dtype=jnp.int32), nbr_layers, count_layers, center, environment),
    )


def fold_dim(ghost_grid, grid_dim, axis_size, send_rim):
    inner_size = ghost_grid.shape[grid_dim] - 4
    lower_rim = lax.slice_in_dim(ghost_grid, 0, 2, axis=grid_dim)
    upper_rim = lax.slice_in_dim(ghost_grid, inner_size + 2, inner_size + 4, axis=grid_dim)
    core_cells = lax.slice_in_dim(ghost_grid, 2, inner_size + 2, axis=grid_dim)
    for rim_cells, hop_count, first_row in (
        (upper_rim, 1, 0),
        (lower_rim, axis_size - 1, inner_size - 2),
    ):
        arrived = send_rim(rim_cells, hop_count)
        current = lax.slice_in_dim(core_cells, first_row, first_row + 2, axis=grid_dim)
        core_cells = lax.dynamic_update_slice_in_dim(
            core_cells, current + arrived, first_row, grid_dim
        )
    return core_cells


def fold_gx(ghost_grid):
    return fold_dim(
        ghost_grid,
        0,
        lax.axis_size("gx"),
        lambda rim_cells, hop_count: passed_along(
            rim_cells.astype(jnp.bfloat16), "gx", hop_count
        ).astype(rim_cells.dtype),
    )


def fold_gy(ghost_grid):
    return fold_dim(
        ghost_grid,
        1,
        lax.axis_size("gy"),
        lambda rim_cells, hop_count: passed_along(
            rim_cells.astype(jnp.bfloat16), "gy", hop_count
        ).astype(rim_cells.dtype),
    )


def fold_gz(ghost_grid):
    return fold_dim(
        ghost_grid,
        2,
        lax.axis_size("gz"),
        lambda rim_cells, hop_count: passed_along(
            rim_cells.astype(jnp.bfloat16), "gz", hop_count
        ).astype(rim_cells.dtype),
    )


def fold_back(ghost_grid):
    return fold_gz(fold_gy(fold_gx(ghost_grid)))


def shards(
    offsets,
    species,
    neighbours,
    counts,
    embed,
    radial_a,
    mix_in,
    proj_center,
    proj_neigh,
    radial_b,
    couple,
    latent_two,
    latent_three,
    readout,
):
    layer_rows = CY * CZ * PER_CELL
    nbr_layers = neighbours.reshape(CX, layer_rows, SLOTS)
    count_layers = counts.reshape(CX, layer_rows)
    species_layers = species.reshape(CX, layer_rows)
    ext_offsets = padded(offsets, (("gx", 0), ("gy", 1), ("gz", 2)), 2)

    def section_env(shell_offsets):
        return brick_environment(
            shell_offsets, nbr_layers, count_layers, species_layers, embed, radial_a, mix_in
        )

    (hidden_full, environment), pull_env = jax.vjp(section_env, ext_offsets)
    hidden = hidden_full.astype(jnp.bfloat16)
    hidden_grid = hidden.reshape(CX, CY, CZ, PER_CELL, CH)
    ext_hidden = padded(hidden_grid, (("gx", 0), ("gy", 1), ("gz", 2)), 2)
    center = jnp.dot(
        hidden.reshape(-1, CH), proj_center, preferred_element_type=jnp.float32
    ).reshape(hidden.shape)
    neigh_rows = jnp.dot(ext_hidden.reshape(-1, CH), proj_neigh, preferred_element_type=jnp.float32)

    def section_pairs(shell_offsets, center_all, neigh_all, env_all):
        return brick_energy(
            shell_offsets,
            center_all,
            neigh_all,
            env_all,
            nbr_layers,
            count_layers,
            couple,
            radial_b,
            latent_two,
            latent_three,
            readout,
        )

    energy, pull_pairs = jax.vjp(section_pairs, ext_offsets, center, neigh_rows, environment)
    grad_offsets_b, grad_center, grad_neigh, grad_env = pull_pairs(jnp.ones_like(energy))
    neigh_owned = fold_back(grad_neigh.reshape(CX + 4, CY + 4, CZ + 4, PER_CELL, CH))
    from_center = jnp.dot(
        grad_center.reshape(-1, CH),
        proj_center.astype(jnp.float32).T,
        precision=lax.Precision.HIGHEST,
    )
    from_neigh = jnp.dot(
        neigh_owned.reshape(-1, CH),
        proj_neigh.astype(jnp.float32).T,
        precision=lax.Precision.HIGHEST,
    )
    grad_hidden = (from_center + from_neigh).reshape(hidden.shape)
    (grad_offsets_a,) = pull_env((grad_hidden, grad_env))
    owned_grad = fold_back(grad_offsets_a + grad_offsets_b)
    forces = -owned_grad
    return (forces, energy.reshape(CX, CY, CZ, PER_CELL))


def solution(mesh):
    placed = (
        P("gx", "gy", "gz", None, None),
        P("gx", "gy", "gz", None),
        P("gx", "gy", "gz", None, None),
        P("gx", "gy", "gz", None),
        P(),
        P(),
        P(),
        P(),
        P(),
        P(),
        P(),
        P(),
        P(),
        P(),
    )
    return jax.shard_map(
        shards,
        mesh=mesh,
        in_specs=placed,
        out_specs=(P("gx", "gy", "gz", None, None), P("gx", "gy", "gz", None)),
        check_vma=False,
    )
```

profile of v0, /device:TPU:6, one launch (start us, length us, event | category | flops | bytes accessed | tf_op | source)
XLA Modules:
  0.0 1885.2 jit_solution(6815480059992001322)
XLA Ops:
  33.9 191.3 %while.72 = (s32[]{:T(128)}, bf16[4,128,128]{2,1,0:T(8,128)(2,1)}, f32[4,9,128,128]{3,1,2,0:T(8,128)}, s32[4,128]{1,0:T(4,128)S(1)}, s32[4,128,32]{1,2,0:T(8,128...) while((s32[]{:T(128)}, bf16[4,128,128]{2,1,0:T(8,128)(2,1)}, ...), condition=%wide.region_4.5_spmd.clone.clone, body=%wide.region_0.4_spmd.clone.clone.sunk | while | flops 122680976 | bytes 11728221 | solution.py:191
  34.6 14.2 gather_fusion.1
  82.3 14.2 gather_fusion.1
  129.9 14.2 gather_fusion.1
  177.5 14.2 gather_fusion.1
  247.0 18.1 collective-permute-done.10
  276.1 736.2 %while.74 = (s32[]{:T(128)}, f32[6144,3]{1,0:T(8,128)}, f32[6144,128]{1,0:T(8,128)}, f32[4,128,128]{2,1,0:T(8,128)}, f32[4,9,128,128]{3,1,2,0:T(8,128)}, /*index...) while((s32[]{:T(128)}, f32[6144,3]{1,0:T(8,128)}, ...), condition=%wide.region_15.16_spmd.clone, body=%wide.region_5.15_spmd.clone.sunk | while | flops 842246528 | bytes 71334384 | solution.py:229
  303.6 14.2 gather_fusion.6
  351.4 16.1 gather_fusion.7
  389.7 9.0 fusion.695
  421.6 24.5 %scatter_custom_fusion.25 = f32[6144,3]{1,0:T(8,128)} fusion(s32[4096]{0:T(1024)S(1)} %reshape.3183, f32[4096,3]{1,0:T(8,128)} %bitcast.871, f32[]{:T(128)} %constant.1331.clone.1..sunk), kind=kCustom, calls=%fused_computation.453.clone.1 | custom fusion | flops 12288 | bytes 74240 | tf_op jit(solution)/shard_map/transpose(jvp())/while/body/eval_jaxpr/checkpoint/scatter-add | solution.py:74
  451.1 24.0 %scatter_fusion = f32[6144,128]{1,0:T(8,128)} fusion(f32[6144,128]{1,0:T(8,128)} %get-tuple-element.2894, s32[4096]{0:T(1024)S(1)} %reshape.3183, f32[4096,128]{1,0:T(8,128)} %bitcast.867), kind=kCustom, calls=%fused_computation.12.clone.clone.1 | custom fusion | flops 524288 | bytes 6307840 | tf_op jit(solution)/shard_map/transpose(jvp())/while/body/eval_jaxpr/checkpoint/scatter-add | solution.py:146
  480.4 14.2 gather_fusion.6
  528.1 16.1 gather_fusion.7
  566.5 9.0 fusion.695
  598.4 24.5 %scatter_custom_fusion.25 = f32[6144,3]{1,0:T(8,128)} fusion(s32[4096]{0:T(1024)S(1)} %reshape.3183, f32[4096,3]{1,0:T(8,128)} %bitcast.871, f32[]{:T(128)} %constant.1331.clone.1..sunk), kind=kCustom, calls=%fused_computation.453.clone.1 | custom fusion | flops 12288 | bytes 74240 | tf_op jit(solution)/shard_map/transpose(jvp())/while/body/eval_jaxpr/checkpoint/scatter-add | solution.py:74
  628.8 24.0 %scatter_fusion = f32[6144,128]{1,0:T(8,128)} fusion(f32[6144,128]{1,0:T(8,128)} %get-tuple-element.2894, s32[4096]{0:T(1024)S(1)} %reshape.3183, f32[4096,128]{1,0:T(8,128)} %bitcast.867), kind=kCustom, calls=%fused_computation.12.clone.clone.1 | custom fusion | flops 524288 | bytes 6307840 | tf_op jit(solution)/shard_map/transpose(jvp())/while/body/eval_jaxpr/checkpoint/scatter-add | solution.py:146
  658.0 14.2 gather_fusion.6
  705.8 16.1 gather_fusion.7
  721.9 8.0 multiply_convert_fusion.28
  744.1 9.0 fusion.695
  776.0 24.5 %scatter_custom_fusion.25 = f32[6144,3]{1,0:T(8,128)} fusion(s32[4096]{0:T(1024)S(1)} %reshape.3183, f32[4096,3]{1,0:T(8,128)} %bitcast.871, f32[]{:T(128)} %constant.1331.clone.1..sunk), kind=kCustom, calls=%fused_computation.453.clone.1 | custom fusion | flops 12288 | bytes 74240 | tf_op jit(solution)/shard_map/transpose(jvp())/while/body/eval_jaxpr/checkpoint/scatter-add | solution.py:74
  806.4 24.0 %scatter_fusion = f32[6144,128]{1,0:T(8,128)} fusion(f32[6144,128]{1,0:T(8,128)} %get-tuple-element.2894, s32[4096]{0:T(1024)S(1)} %reshape.3183, f32[4096,128]{1,0:T(8,128)} %bitcast.867), kind=kCustom, calls=%fused_computation.12.clone.clone.1 | custom fusion | flops 524288 | bytes 6307840 | tf_op jit(solution)/shard_map/transpose(jvp())/while/body/eval_jaxpr/checkpoint/scatter-add | solution.py:146
  835.6 14.2 gather_fusion.6
  883.4 16.1 gather_fusion.7
  899.5 8.0 multiply_convert_fusion.28
  921.8 9.0 fusion.695
  953.7 24.5 %scatter_custom_fusion.25 = f32[6144,3]{1,0:T(8,128)} fusion(s32[4096]{0:T(1024)S(1)} %reshape.3183, f32[4096,3]{1,0:T(8,128)} %bitcast.871, f32[]{:T(128)} %constant.1331.clone.1..sunk), kind=kCustom, calls=%fused_computation.453.clone.1 | custom fusion | flops 12288 | bytes 74240 | tf_op jit(solution)/shard_map/transpose(jvp())/while/body/eval_jaxpr/checkpoint/scatter-add | solution.py:74
  984.0 24.0 %scatter_fusion = f32[6144,128]{1,0:T(8,128)} fusion(f32[6144,128]{1,0:T(8,128)} %get-tuple-element.2894, s32[4096]{0:T(1024)S(1)} %reshape.3183, f32[4096,128]{1,0:T(8,128)} %bitcast.867), kind=kCustom, calls=%fused_computation.12.clone.clone.1 | custom fusion | flops 524288 | bytes 6307840 | tf_op jit(solution)/shard_map/transpose(jvp())/while/body/eval_jaxpr/checkpoint/scatter-add | solution.py:146
  1018.0 8.9 collective-permute-done.12
  1049.0 479.0 %while.75 = (s32[]{:T(128)}, f32[6144,3]{1,0:T(8,128)}, s32[4]{0:T(128)S(1)}, s32[4,128,32]{1,2,0:T(8,128)S(1)}, s32[4,128]{1,0:T(4,128)S(1)}, /*index=5*/s32[4,...) while((s32[]{:T(128)}, f32[6144,3]{1,0:T(8,128)}, ...), condition=%wide.region_29.30_spmd.clone, body=%wide.region_16.29_spmd.clone.sunk | while | flops 303265152 | bytes 67981760 | solution.py:191
  1054.6 14.2 gather_fusion.9
  1138.7 24.5 %scatter_custom_fusion.30 = f32[6144,3]{1,0:T(8,128)} fusion(s32[4096]{0:T(1024)} %copy-done.26, f32[4096,3]{1,0:T(8,128)} %bitcast.870, f32[]{:T(128)} %constant.1331.clone.1..sunk.1), kind=kCustom, calls=%fused_computation.635.clone.1 | custom fusion | flops 12288 | bytes 74240 | tf_op jit(solution)/shard_map/transpose(jvp())/while/body/eval_jaxpr/checkpoint/scatter-add | solution.py:74
  1173.5 14.2 gather_fusion.9
  1257.6 24.5 %scatter_custom_fusion.30 = f32[6144,3]{1,0:T(8,128)} fusion(s32[4096]{0:T(1024)} %copy-done.26, f32[4096,3]{1,0:T(8,128)} %bitcast.870, f32[]{:T(128)} %constant.1331.clone.1..sunk.1), kind=kCustom, calls=%fused_computation.635.clone.1 | custom fusion | flops 12288 | bytes 74240 | tf_op jit(solution)/shard_map/transpose(jvp())/while/body/eval_jaxpr/checkpoint/scatter-add | solution.py:74
  1293.3 14.2 gather_fusion.9
  1377.4 24.5 %scatter_custom_fusion.30 = f32[6144,3]{1,0:T(8,128)} fusion(s32[4096]{0:T(1024)} %copy-done.26, f32[4096,3]{1,0:T(8,128)} %bitcast.870, f32[]{:T(128)} %constant.1331.clone.1..sunk.1), kind=kCustom, calls=%fused_computation.635.clone.1 | custom fusion | flops 12288 | bytes 74240 | tf_op jit(solution)/shard_map/transpose(jvp())/while/body/eval_jaxpr/checkpoint/scatter-add | solution.py:74
  1413.1 14.2 gather_fusion.9
  1497.2 24.5 %scatter_custom_fusion.30 = f32[6144,3]{1,0:T(8,128)} fusion(s32[4096]{0:T(1024)} %copy-done.26, f32[4096,3]{1,0:T(8,128)} %bitcast.870, f32[]{:T(128)} %constant.1331.clone.1..sunk.1), kind=kCustom, calls=%fused_computation.635.clone.1 | custom fusion | flops 12288 | bytes 74240 | tf_op jit(solution)/shard_map/transpose(jvp())/while/body/eval_jaxpr/checkpoint/scatter-add | solution.py:74
  1560.0 322.6 %while.73 = (s32[]{:T(128)}, f32[4,128]{1,0:T(4,128)S(1)}, s32[4,128]{1,0:T(4,128)S(1)}, s32[4,128,32]{1,2,0:T(8,128)S(1)}, s32[4]{0:T(128)S(1)}, /*index=5*/f32...) while((s32[]{:T(128)}, f32[4,128]{1,0:T(4,128)S(1)}, ...), condition=%wide.region_32.33_spmd.clone.clone, body=%wide.region_30.32_spmd.clone.clone.sunk | while | flops 391988096 | bytes 21481288 | solution.py:229
  1560.4 14.2 gather_fusion.3
  1608.0 16.1 gather_fusion.4
  1641.0 14.2 gather_fusion.3
  1688.6 16.1 gather_fusion.4
  1721.6 14.2 gather_fusion.3
  1769.2 16.1 gather_fusion.4
  1802.2 14.2 gather_fusion.3
  1849.8 16.1 gather_fusion.4
  (1353 shorter events, 1116.0 us)
Async XLA Ops:
  0.6 268.4 %copy-start = (bf16[128,128]{1,0:T(8,128)(2,1)S(1)}, bf16[128,128]{1,0:T(8,128)(2,1)}, u32[]{:S(2)}) copy-start(bf16[128,128]{1,0:T(8,128)(2,1)} %param.30) | copy-start | bytes 98308
  1.4 4.9 collective-permute-start
  1.5 5.6 collective-permute-start.1
  7.2 4.2 collective-permute-start.2
  7.8 5.3 collective-permute-start.3
  13.2 11.3 collective-permute-start.4
  15.1 11.8 collective-permute-start.5
  225.3 43.7 %copy-start.53 = (s32[4,128]{1,0:T(4,128)}, s32[4,128]{1,0:T(4,128)S(1)}, u32[]{:S(2)}) copy-start(s32[4,128]{1,0:T(4,128)S(1)} %get-tuple-element.3120) | copy-start | bytes 6148
  226.2 5.3 collective-permute-start.6
  226.3 5.2 collective-permute-start.7
  232.4 6.4 collective-permute-start.8
  232.8 7.4 collective-permute-start.9
  242.0 23.1 %collective-permute-start.10 = (bf16[8,8,2,16,128]{4,3,2,1,0:T(8,128)(2,1)}, bf16[8,8,2,16,128]{4,3,2,1,0:T(8,128)(2,1)}, u32[]{:S(2)}, u32[]{:S(2)}) collective-permute-start(bf16[8,8,2,16,128]{4,3,2,1,0:T(8,128)(2,1)} %pad_maximum_fusion.6), channel_id=1, source_target_pairs={{0,1},{1,2},{2,3},{3,4},{4,5},{5,6},{6,7},{7,0},{8,9},{9,10},{10,1... | collective-permute-start | bytes 1572872 | tf_op jit(solution)/shard_map/ppermute | solution.py:36
  242.0 25.5 %collective-permute-start.11 = (bf16[8,8,2,16,128]{4,3,2,1,0:T(8,128)(2,1)}, bf16[8,8,2,16,128]{4,3,2,1,0:T(8,128)(2,1)}, u32[]{:S(2)}, u32[]{:S(2)}) collective-permute-start(bf16[8,8,2,16,128]{4,3,2,1,0:T(8,128)(2,1)} %pad_maximum_fusion.6), channel_id=1, source_target_pairs={{1,0},{2,1},{3,2},{4,3},{5,4},{6,5},{7,6},{0,7},{9,8},{10,9},{11,1... | collective-permute-start | bytes 1572872 | tf_op jit(solution)/shard_map/ppermute | solution.py:37
  303.4 39.2 %copy-start.44 = (s32[128]{0:T(128)}, s32[128]{0:T(128)S(1)}, u32[]{:S(2)}) copy-start(s32[128]{0:T(128)S(1)} %fusion.685) | copy-start | bytes 1540 | tf_op jit(solution)/shard_map/transpose(jvp())/while
  451.1 24.7 %copy-start.34 = (f32[8,128]{1,0:T(8,128)S(1)}, f32[8,128]{1,0:T(8,128)}, u32[]{:S(2)}) copy-start(f32[8,128]{1,0:T(8,128)} %get-tuple-element.3082) | copy-start | bytes 12292 | tf_op jit(solution)/shard_map/transpose(jvp())/while
  451.1 24.7 %copy-start.50 = (s32[4,128]{1,0:T(4,128)S(1)}, s32[4,128]{1,0:T(4,128)}, u32[]{:S(2)}) copy-start(s32[4,128]{1,0:T(4,128)} %copy-done.49) | copy-start | bytes 6148 | tf_op jit(solution)/shard_map/transpose(jvp())/while
  451.1 24.7 %copy-start.61 = (f32[128]{0:T(128)S(1)}, f32[128]{0:T(128)}, u32[]{:S(2)}) copy-start(f32[128]{0:T(128)} %get-tuple-element.3152) | copy-start | bytes 1540 | tf_op jit(solution)/shard_map/transpose(jvp())/while
  451.1 24.6 %copy-start.64 = (s32[4]{0:T(128)S(1)}, s32[4]{0:T(128)}, u32[]{:S(2)}) copy-start(s32[4]{0:T(128)} %copy-done.63) | copy-start | bytes 52 | tf_op jit(solution)/shard_map/transpose(jvp())/while
  480.1 39.2 %copy-start.44 = (s32[128]{0:T(128)}, s32[128]{0:T(128)S(1)}, u32[]{:S(2)}) copy-start(s32[128]{0:T(128)S(1)} %fusion.685) | copy-start | bytes 1540 | tf_op jit(solution)/shard_map/transpose(jvp())/while
  628.8 24.6 %copy-start.50 = (s32[4,128]{1,0:T(4,128)S(1)}, s32[4,128]{1,0:T(4,128)}, u32[]{:S(2)}) copy-start(s32[4,128]{1,0:T(4,128)} %copy-done.49) | copy-start | bytes 6148 | tf_op jit(solution)/shard_map/transpose(jvp())/while
  628.8 24.6 %copy-start.61 = (f32[128]{0:T(128)S(1)}, f32[128]{0:T(128)}, u32[]{:S(2)}) copy-start(f32[128]{0:T(128)} %get-tuple-element.3152) | copy-start | bytes 1540 | tf_op jit(solution)/shard_map/transpose(jvp())/while
  657.8 39.2 %copy-start.44 = (s32[128]{0:T(128)}, s32[128]{0:T(128)S(1)}, u32[]{:S(2)}) copy-start(s32[128]{0:T(128)S(1)} %fusion.685) | copy-start | bytes 1540 | tf_op jit(solution)/shard_map/transpose(jvp())/while
  806.4 24.6 %copy-start.34 = (f32[8,128]{1,0:T(8,128)S(1)}, f32[8,128]{1,0:T(8,128)}, u32[]{:S(2)}) copy-start(f32[8,128]{1,0:T(8,128)} %get-tuple-element.3082) | copy-start | bytes 12292 | tf_op jit(solution)/shard_map/transpose(jvp())/while
  806.4 24.6 %copy-start.50 = (s32[4,128]{1,0:T(4,128)S(1)}, s32[4,128]{1,0:T(4,128)}, u32[]{:S(2)}) copy-start(s32[4,128]{1,0:T(4,128)} %copy-done.49) | copy-start | bytes 6148 | tf_op jit(solution)/shard_map/transpose(jvp())/while
  806.4 24.6 %copy-start.61 = (f32[128]{0:T(128)S(1)}, f32[128]{0:T(128)}, u32[]{:S(2)}) copy-start(f32[128]{0:T(128)} %get-tuple-element.3152) | copy-start | bytes 1540 | tf_op jit(solution)/shard_map/transpose(jvp())/while
  806.4 24.6 %copy-start.64 = (s32[4]{0:T(128)S(1)}, s32[4]{0:T(128)}, u32[]{:S(2)}) copy-start(s32[4]{0:T(128)} %copy-done.63) | copy-start | bytes 52 | tf_op jit(solution)/shard_map/transpose(jvp())/while
  835.4 39.2 %copy-start.44 = (s32[128]{0:T(128)}, s32[128]{0:T(128)S(1)}, u32[]{:S(2)}) copy-start(s32[128]{0:T(128)S(1)} %fusion.685) | copy-start | bytes 1540 | tf_op jit(solution)/shard_map/transpose(jvp())/while
  984.0 24.6 %copy-start.34 = (f32[8,128]{1,0:T(8,128)S(1)}, f32[8,128]{1,0:T(8,128)}, u32[]{:S(2)}) copy-start(f32[8,128]{1,0:T(8,128)} %get-tuple-element.3082) | copy-start | bytes 12292 | tf_op jit(solution)/shard_map/transpose(jvp())/while
  984.0 24.6 %copy-start.50 = (s32[4,128]{1,0:T(4,128)S(1)}, s32[4,128]{1,0:T(4,128)}, u32[]{:S(2)}) copy-start(s32[4,128]{1,0:T(4,128)} %copy-done.49) | copy-start | bytes 6148 | tf_op jit(solution)/shard_map/transpose(jvp())/while
  984.0 24.6 %copy-start.61 = (f32[128]{0:T(128)S(1)}, f32[128]{0:T(128)}, u32[]{:S(2)}) copy-start(f32[128]{0:T(128)} %get-tuple-element.3152) | copy-start | bytes 1540 | tf_op jit(solution)/shard_map/transpose(jvp())/while
  984.0 24.6 %copy-start.64 = (s32[4]{0:T(128)S(1)}, s32[4]{0:T(128)}, u32[]{:S(2)}) copy-start(s32[4]{0:T(128)} %copy-done.63) | copy-start | bytes 52 | tf_op jit(solution)/shard_map/transpose(jvp())/while
  1014.5 12.4 collective-permute-start.12
  1014.6 12.4 collective-permute-start.13
  1029.2 7.5 collective-permute-start.14
  1032.1 7.8 collective-permute-start.15
  1040.0 7.3 collective-permute-start.16
  1040.1 7.9 collective-permute-start.17
  1050.0 38.0 %copy-start.43 = (s32[128]{0:T(128)}, s32[128]{0:T(128)S(1)}, u32[]{:S(2)}) copy-start(s32[128]{0:T(128)S(1)} %get-tuple-element.2795) | copy-start | bytes 1540 | tf_op jit(solution)/shard_map/transpose(jvp())/while
  1168.9 38.0 %copy-start.43 = (s32[128]{0:T(128)}, s32[128]{0:T(128)S(1)}, u32[]{:S(2)}) copy-start(s32[128]{0:T(128)S(1)} %get-tuple-element.2795) | copy-start | bytes 1540 | tf_op jit(solution)/shard_map/transpose(jvp())/while
  1288.7 38.0 %copy-start.43 = (s32[128]{0:T(128)}, s32[128]{0:T(128)S(1)}, u32[]{:S(2)}) copy-start(s32[128]{0:T(128)S(1)} %get-tuple-element.2795) | copy-start | bytes 1540 | tf_op jit(solution)/shard_map/transpose(jvp())/while
  1408.5 38.0 %copy-start.43 = (s32[128]{0:T(128)}, s32[128]{0:T(128)S(1)}, u32[]{:S(2)}) copy-start(s32[128]{0:T(128)S(1)} %get-tuple-element.2795) | copy-start | bytes 1540 | tf_op jit(solution)/shard_map/transpose(jvp())/while
  1539.7 5.6 collective-permute-start.18
  1540.9 5.5 collective-permute-start.19
  1547.2 4.5 collective-permute-start.20
  1549.0 5.5 collective-permute-start.21
  1555.9 327.4 %collective-permute-start.22 = (bf16[4,4,2,3,16]{4,2,1,0,3:T(2,128)(2,1)}, bf16[4,4,2,3,16]{4,2,1,0,3:T(2,128)(2,1)S(1)}, u32[]{:S(2)}, u32[]{:S(2)}) collective-permute-start(bf16[4,4,2,3,16]{4,2,1,0,3:T(2,128)(2,1)} %get-tuple-element.2235), channel_id=1, source_target_pairs={{7,0},{0,1},{1,2},{2,3},{3,4},{4,5},{5,6},{6,7},{15,8},{8,9},{9,10... | collective-permute-start | bytes 9224 | tf_op jit(solution)/shard_map/ppermute | solution.py:26
  1556.1 327.2 %collective-permute-start.23 = (bf16[4,4,2,3,16]{4,2,1,0,3:T(2,128)(2,1)}, bf16[4,4,2,3,16]{4,2,1,0,3:T(2,128)(2,1)}, u32[]{:S(2)}, u32[]{:S(2)}) collective-permute-start(bf16[4,4,2,3,16]{4,2,1,0,3:T(2,128)(2,1)} %get-tuple-element.2236), channel_id=1, source_target_pairs={{1,0},{2,1},{3,2},{4,3},{5,4},{6,5},{7,6},{0,7},{9,8},{10,9},{11,1... | collective-permute-start | bytes 9224 | tf_op jit(solution)/shard_map/ppermute | solution.py:26
  (181 other events, 1141.8 us)
where the time goes:
time: 1900 us; the launch traced here: 1890 us
  local copies, waits for them, and re-layouts  826 us (43%)
  other arithmetic  485 us (26%)
  matrix products  430 us (23%)
  waiting for transfers between devices  62.3 us (3%)
  loops' own time  41.8 us (2%)
  starting transfers between devices  38.8 us (2%)
    gather x16, local copies, waits for them, and re-layouts, layer_geometry(): other_place = flat_offsets[layer_nbr]  227 us
    scatter-add x8, other arithmetic, layer_geometry(): other_place = flat_offsets[layer_nbr]  196 us
    while x432, local copies, waits for them, and re-layouts  148 us
    gather x8, local copies, waits for them, and re-layouts, layer_energy(): gathered = neigh_rows[layer_nbr]  129 us
    slice x16, local copies, waits for them, and re-layouts, layer_geometry(): other_place[:, :, 0]  108 us
    dot_general x16, matrix products, layer_energy(): jnp.einsum('mak,mac->akc', harmonic_values, environment * couple_full[:,...  107 us
    scatter-add x4, other arithmetic, layer_energy(): gathered = neigh_rows[layer_nbr]  95.9 us
    dot_general x12, matrix products, layer_energy(): jnp.einsum('akn,nc->akc', bessel, radial_b, precision=lax.Precision.HIGHEST)  82.8 us
  transfers between devices with their start and end apart: 24, of which 19 were waited for; matrix products, arithmetic and copies ran while one was open for 18% of the time, Pallas kernels for 0%

commit v1 on v0

v1 whole, which is shorter than its diff:
```python
import math

import jax
import jax.numpy as jnp
from jax import lax
from jax.experimental import pallas as pl
from jax.experimental.pallas import tpu as pltpu
from jax.sharding import PartitionSpec as P

CX = 4
CY = 4
CZ = 2
PER_CELL = 16
SLOTS = 32
CH = 128
NBASIS = 8
SPECIES = 4

CELL_SIDE = 2.0
CUTOFF = 10.5
NORM_EPS = 1e-05

COLS = CX * CY
PAIRS = CZ * PER_CELL * SLOTS
CELL_PAIRS = PER_CELL * SLOTS
ATOMS = COLS * CZ * PER_CELL
RUN = 48
SLAB = 5 * RUN
CELL_ROWS = 40

F32 = jnp.float32
BF16 = jnp.bfloat16
DEGREE = (0, 1, 1, 1, 2, 2, 2, 2, 2)

F_Y = 0
F_W = 9
F_DW = 10
F_B = 11
F_DB = 19
F_INV = 27
F_COUNT = 28

G_B = 0
G_Y = 8
G_E = 17
G_COUNT = 24


def dims(a, b, ca, cb):
    return lax.dot_general(a, b, (((ca,), (cb,)), ((), ())), preferred_element_type=F32)


def halves(value):
    high = value.astype(BF16)
    return high, (value - high.astype(F32)).astype(BF16)


def dims_three(a, b, ca, cb):
    a_high, a_low = halves(a)
    b_high, b_low = halves(b)
    return dims(a_high, b_high, ca, cb) + (
        dims(a_high, b_low, ca, cb) + dims(a_low, b_high, ca, cb)
    )


def iota(shape, dim):
    return lax.broadcasted_iota(jnp.int32, shape, dim)


def one_hot(condition):
    return jnp.where(condition, 1.0, 0.0).astype(BF16)


def radial_blocks(radial):
    rows = []
    for m in range(9):
        before = [jnp.zeros((NBASIS, m * CH), F32)] if m else []
        after = [jnp.zeros((NBASIS, (8 - m) * CH), F32)] if m < 8 else []
        rows.append(jnp.concatenate(before + [radial] + after, 1))
    return jnp.concatenate(rows, 0)


def sigmoid_of(v):
    return 0.5 * jnp.tanh(0.5 * v) + 0.5


def feature_rows(ref, row, count, i):
    blocks = []
    for lane in range(PAIRS // 128):
        start = (lane * F_COUNT + row) * COLS + i
        blocks.append(ref[pl.ds(start, count, stride=COLS) if count > 1 else pl.ds(start, 1), :])
    return jnp.concatenate(blocks, 1)


def whole_feature(ref, row):
    blocks = []
    for lane in range(PAIRS // 128):
        start = (lane * F_COUNT + row) * COLS
        blocks.append(ref[start : start + COLS, :])
    return jnp.concatenate(blocks, 1)


def put_feature(ref, row, value):
    for lane in range(PAIRS // 128):
        start = (lane * F_COUNT + row) * COLS
        ref[start : start + COLS, :] = value[:, lane * 128 : (lane + 1) * 128]


def cell_window(ref, x, y):
    parts = []
    for dx in range(5):
        start = pl.multiple_of(((x + dx) * 8 + y) * 8, 8)
        parts.append(ref[pl.ds(start, CELL_ROWS), :])
    return jnp.concatenate(parts, 0)


def env_kernel(
    nbr_ref,
    ext_ref,
    own_ref,
    count_ref,
    species_ref,
    embed_ref,
    radial_ref,
    mix_ref,
    hidden_ref,
    env_ref,
    scale_ref,
    feat_ref,
    code_ref,
    near_ref,
    moment_ref,
):
    shape = (COLS, PAIRS)
    number = nbr_ref[...]
    slot = number & 15
    cell = number >> 4
    over = (cell * 43691) >> 18
    cell_z = cell - 6 * over
    cell_y = over & 7
    cell_x = over >> 3
    column = iota(shape, 0)
    lane = iota(shape, 1)
    dx = cell_x - (column >> 2)
    dy = cell_y - (column & 3)
    upper = (cell_z >= 3).astype(jnp.int32)
    code_ref[0] = (dx * 5 + dy) * RUN + (cell_z - 3 * upper) * PER_CELL + slot
    code_ref[1] = upper
    code_ref[2] = dx * CELL_ROWS + dy * 8 + cell_z
    code_ref[3] = slot

    row_cells = iota((5 * CELL_ROWS, PAIRS), 0)
    row_slots = iota((PER_CELL, PAIRS), 0)

    def fetch(i, carry):
        hot = one_hot(row_cells == code_ref[2, pl.ds(i, 1), :])
        high, low = halves(cell_window(ext_ref, i // CY, i % CY))
        places = dims(high, hot, 0, 0) + dims(low, hot, 0, 0)
        mask = row_slots == code_ref[3, pl.ds(i, 1), :]
        for c in range(3):
            part = places[c * PER_CELL : (c + 1) * PER_CELL]
            near_ref[c, pl.ds(i, 1), :] = jnp.sum(jnp.where(mask, part, 0.0), 0, keepdims=True)
        return carry

    lax.fori_loop(0, COLS, fetch, 0)

    spread = one_hot(iota((32, PAIRS), 0) == (iota((32, PAIRS), 1) >> 5))
    own_high, own_low = halves(own_ref[...])
    own = dims(own_high, spread, 1, 0) + dims(own_low, spread, 1, 0)
    count = dims(count_ref[...].astype(F32).astype(BF16), spread, 1, 0)
    live = ((lane & 31).astype(F32) < count).astype(F32)
    step_x = (dx - 2).astype(F32) * CELL_SIDE + near_ref[0] - own[0:COLS]
    step_y = (dy - 2).astype(F32) * CELL_SIDE + near_ref[1] - own[COLS : 2 * COLS]
    step_z = (
        (cell_z - 2 - (lane >> 9)).astype(F32) * CELL_SIDE + near_ref[2] - own[2 * COLS : 3 * COLS]
    )
    square = step_x * step_x + step_y * step_y + step_z * step_z
    distance = jnp.sqrt(square)
    inverse = 1.0 / distance
    nx, ny, nz = step_x * inverse, step_y * inverse, step_z * inverse

    def put(row, value):
        put_feature(feat_ref, row, value)

    three, five, fifteen = math.sqrt(3.0), math.sqrt(5.0), math.sqrt(15.0)
    put(F_Y, jnp.ones(shape, F32))
    put(F_Y + 1, three * nx)
    put(F_Y + 2, three * ny)
    put(F_Y + 3, three * nz)
    put(F_Y + 4, fifteen * nx * ny)
    put(F_Y + 5, fifteen * ny * nz)
    put(F_Y + 6, (0.5 * five) * (3.0 * nz * nz - 1.0))
    put(F_Y + 7, fifteen * nx * nz)
    put(F_Y + 8, (0.5 * fifteen) * (nx * nx - ny * ny))
    scaled = distance * (1.0 / CUTOFF)
    inside = 1.0 - scaled * scaled
    put(F_W, live * inside * inside)
    put(F_DW, live * (-4.0 / CUTOFF) * scaled * inside)
    put(F_INV, inverse)
    angle = distance * (math.pi / CUTOFF)
    sine, cosine = jnp.sin(angle), jnp.cos(angle)
    last_s, last_c = jnp.zeros(shape, F32), jnp.ones(shape, F32)
    now_s, now_c = sine, cosine
    for k in range(1, NBASIS + 1):
        basis = CELL_SIDE * now_s * inverse
        put(F_B + k - 1, basis)
        put(F_DB + k - 1, (CELL_SIDE * k * math.pi / CUTOFF * now_c - basis) * inverse)
        last_s, now_s = now_s, 2.0 * cosine * now_s - last_s
        last_c, now_c = now_c, 2.0 * cosine * now_c - last_c

    atoms = one_hot(iota((PER_CELL, CELL_PAIRS), 0) == (iota((PER_CELL, CELL_PAIRS), 1) >> 5))

    def moments(i, carry):
        harmonic = feature_rows(feat_ref, F_Y, 9, i)
        weighted = feature_rows(feat_ref, F_B, NBASIS, i) * feature_rows(feat_ref, F_W, 1, i)
        products = jnp.concatenate([harmonic[m : m + 1] * weighted for m in range(9)], 0)
        high, low = halves(products)
        for z in range(CZ):
            part = slice(z * CELL_PAIRS, (z + 1) * CELL_PAIRS)
            start = pl.multiple_of((i * CZ + z) * PER_CELL, PER_CELL)
            moment_ref[pl.ds(start, PER_CELL), :] = dims(atoms, high[:, part], 1, 1) + dims(
                atoms, low[:, part], 1, 1
            )
        return carry

    lax.fori_loop(0, COLS, moments, 0)

    kind = one_hot(iota((SPECIES, ATOMS), 0) == species_ref[...])
    embed_high, embed_low = halves(embed_ref[...] * (1.0 / math.sqrt(SLOTS)))
    scale = dims(kind, embed_high, 0, 0) + dims(kind, embed_low, 0, 0)
    scale_ref[...] = scale
    sums = dims_three(moment_ref[...], radial_blocks(radial_ref[...]), 1, 0)
    invariants = [None] * 3
    for m in range(9):
        value = sums[:, m * CH : (m + 1) * CH] * scale
        env_ref[m] = value
        degree = DEGREE[m]
        squared = value * value
        invariants[degree] = (
            squared if invariants[degree] is None else invariants[degree] + squared
        )
    normed, _ = normalised(invariants)
    mixed = dims(jnp.concatenate(normed, 1).astype(BF16), mix_ref[...], 1, 0)
    hidden_ref[...] = (mixed * sigmoid_of(mixed)).astype(BF16)


def normalised(invariants):
    total = sum(jnp.sum(q * q, 1, keepdims=True) for q in invariants)
    inverse = lax.rsqrt(total * (1.0 / (3 * CH)) + NORM_EPS)
    return [q * inverse for q in invariants], inverse


def pair_kernel(
    around_ref,
    hidden_ref,
    env_ref,
    feat_ref,
    code_ref,
    center_ref,
    neigh_ref,
    radial_ref,
    couple_ref,
    two_ref,
    three_ref,
    readout_ref,
    energy_ref,
    ghost_ref,
    grad_center_ref,
    grad_env_ref,
    grad_ref,
    table_ref,
    total_ref,
    hot_ref,
    own_ref,
    pair_ref,
):
    for h in range(2):
        rows = around_ref[:, h].reshape(64 * RUN, CH)
        table_ref[:, h * CH : (h + 1) * CH] = dims(rows, neigh_ref[...], 1, 0).astype(BF16)
    total_ref[...] = jnp.zeros_like(total_ref)
    own_ref[...] = dims(hidden_ref[...], center_ref[...], 1, 0)
    readout = jnp.transpose(jnp.broadcast_to(readout_ref[...], (CH, CH)))
    readout = jnp.concatenate([readout] * (PAIRS // CH), 1)
    radial_high, radial_low = halves(radial_ref[...])
    atom_mask = iota((PER_CELL, CELL_PAIRS), 0) == (iota((PER_CELL, CELL_PAIRS), 1) >> 5)
    atoms = one_hot(atom_mask)
    row_slab = iota((SLAB, PAIRS), 0)

    def column(i, carry):
        x, y = i // CY, i % CY
        harmonic = feature_rows(feat_ref, F_Y, 9, i)
        basis_high, basis_low = halves(feature_rows(feat_ref, F_B, NBASIS, i))
        weight = feature_rows(feat_ref, F_W, 1, i)
        code = code_ref[0, pl.ds(i, 1), :]
        upper = code_ref[1, pl.ds(i, 1), :] > 0

        features, tables, parts = [], [], []
        for z in range(CZ):
            part = slice(z * CELL_PAIRS, (z + 1) * CELL_PAIRS)
            start = pl.multiple_of((i * CZ + z) * PER_CELL, PER_CELL)
            blocks = [
                jnp.where(atom_mask, harmonic[m : m + 1, part], 0.0).astype(BF16) for m in range(9)
            ]
            feature = jnp.concatenate(
                blocks
                + [
                    atoms,
                    atoms,
                    basis_high[:, part],
                    basis_low[:, part],
                    basis_high[:, part],
                    jnp.zeros((8, CELL_PAIRS), BF16),
                ],
                0,
            )
            scaled = [
                (env_ref[m, pl.ds(start, PER_CELL), :] * couple_ref[DEGREE[m] : DEGREE[m] + 1]).astype(
                    BF16
                )
                for m in range(9)
            ]
            own_high, own_low = halves(own_ref[pl.ds(start, PER_CELL), :])
            table = jnp.concatenate(
                scaled
                + [
                    own_high,
                    own_low,
                    radial_high,
                    radial_high,
                    radial_low,
                    jnp.zeros((8, CH), BF16),
                ],
                0,
            )
            features.append(feature)
            tables.append(table)
            parts.append(dims(table, feature, 0, 0))
        fetched = None
        for dx in range(5):
            hot = one_hot(row_slab == code - dx * SLAB)
            hot_ref[dx * SLAB : (dx + 1) * SLAB, :] = hot
            rows = pl.multiple_of(((x + dx) * 8 + y) * RUN, RUN)
            found = dims(table_ref[pl.ds(rows, SLAB), :], hot, 0, 0)
            fetched = found if fetched is None else fetched + found
        value = jnp.concatenate(parts, 1) + jnp.where(upper, fetched[CH:], fetched[:CH])
        gate = sigmoid_of(value)
        one = value * gate
        slope_one = gate + one - one * gate
        value = dims(two_ref[...], one.astype(BF16), 0, 0)
        gate = sigmoid_of(value)
        two = value * gate
        slope_two = gate + two - two * gate
        value = dims(three_ref[...], two.astype(BF16), 0, 0)
        gate = sigmoid_of(value)
        top = value * gate
        slope_top = gate + top - top * gate
        pair_energy = jnp.sum(top * readout, 0, keepdims=True)
        pair_ref[pl.ds(i, 1), :] = pair_energy * weight
        grad = slope_top * readout * weight
        grad = dims(three_ref[...], grad.astype(BF16), 1, 0) * slope_two
        grad = dims(two_ref[...], grad.astype(BF16), 1, 0) * slope_one
        spread = jnp.concatenate(
            [jnp.where(upper, 0.0, grad), jnp.where(upper, grad, 0.0)], 0
        ).astype(BF16)
        grad = grad.astype(BF16)
        for dx in range(5):
            rows = pl.multiple_of(((x + dx) * 8 + y) * RUN, RUN)
            total_ref[pl.ds(rows, SLAB), :] += dims(
                hot_ref[dx * SLAB : (dx + 1) * SLAB, :], spread, 1, 1
            )
        for z in range(CZ):
            part = slice(z * CELL_PAIRS, (z + 1) * CELL_PAIRS)
            start = pl.multiple_of((i * CZ + z) * PER_CELL, PER_CELL)
            back = dims(features[z][: 10 * PER_CELL], grad[:, part], 1, 1)
            for m in range(9):
                grad_env_ref[m, pl.ds(start, PER_CELL), :] = back[
                    m * PER_CELL : (m + 1) * PER_CELL
                ]
            grad_center_ref[pl.ds(start, PER_CELL), :] = back[9 * PER_CELL :]
            down = dims(tables[z], grad[:, part], 1, 0)
            for m in range(9):
                kept = jnp.where(atom_mask, down[m * PER_CELL : (m + 1) * PER_CELL], 0.0)
                grad_ref[i, G_Y + m : G_Y + m + 1, part] = jnp.sum(kept, 0, keepdims=True)
            base = 11 * PER_CELL
            grad_ref[i, G_B : G_B + NBASIS, part] = (
                down[base : base + NBASIS] + down[base + 2 * NBASIS : base + 3 * NBASIS]
            )
        grad_ref[i, G_E : G_E + 1, :] = pair_energy
        return carry

    lax.fori_loop(0, COLS, column, 0)
    for h in range(2):
        ghost_ref[:, h] = total_ref[:, h * CH : (h + 1) * CH].astype(BF16).reshape(64, RUN, CH)
    gather = one_hot(iota((32, PAIRS), 0) == (iota((32, PAIRS), 1) >> 5))
    high, low = halves(pair_ref[...])
    energy_ref[...] = dims(high, gather, 1, 1) + dims(low, gather, 1, 1)


def force_kernel(
    neigh_ref,
    grad_center_ref,
    grad_env_ref,
    env_ref,
    scale_ref,
    feat_ref,
    code_ref,
    grad_ref,
    mix_ref,
    center_ref,
    proj_ref,
    radial_ref,
    couple_ref,
    own_ref,
    ghost_ref,
    moment_ref,
    chain_ref,
    pull_ref,
):
    invariants = [None] * 3
    for m in range(9):
        value = env_ref[m]
        squared = value * value
        degree = DEGREE[m]
        invariants[degree] = (
            squared if invariants[degree] is None else invariants[degree] + squared
        )
    normed, inverse = normalised(invariants)
    mixed = dims(jnp.concatenate(normed, 1).astype(BF16), mix_ref[...], 1, 0)
    gate = sigmoid_of(mixed)
    act = mixed * gate
    high, low = halves(grad_center_ref[...])
    grad = dims(high, center_ref[...], 1, 1) + dims(low, center_ref[...], 1, 1)
    high, low = halves(neigh_ref[...])
    grad = grad + dims(high, proj_ref[...], 1, 1) + dims(low, proj_ref[...], 1, 1)
    grad = grad * (gate + act - act * gate)
    grad = dims(grad.astype(BF16), mix_ref[...], 1, 1)
    grads = [grad[:, d * CH : (d + 1) * CH] for d in range(3)]
    mean = sum(jnp.sum(g * q, 1, keepdims=True) for g, q in zip(grads, normed)) * (1.0 / (3 * CH))
    grads = [2.0 * inverse * (g - q * mean) for g, q in zip(grads, normed)]
    scale = scale_ref[...]
    pulled = []
    for m in range(9):
        d = DEGREE[m]
        pulled.append(
            (grad_env_ref[m] * couple_ref[d : d + 1] + env_ref[m] * grads[d]) * scale
        )
    moment_ref[...] = dims_three(
        jnp.concatenate(pulled, 1), radial_blocks(radial_ref[...]), 1, 1
    )

    atoms = one_hot(iota((PER_CELL, CELL_PAIRS), 0) == (iota((PER_CELL, CELL_PAIRS), 1) >> 5))

    def column(i, carry):
        harmonic = feature_rows(feat_ref, F_Y, 9, i)
        basis = feature_rows(feat_ref, F_B, NBASIS, i)
        slope = feature_rows(feat_ref, F_DB, NBASIS, i)
        weight = feature_rows(feat_ref, F_W, 1, i)
        weight_slope = feature_rows(feat_ref, F_DW, 1, i)
        parts = []
        for z in range(CZ):
            start = pl.multiple_of((i * CZ + z) * PER_CELL, PER_CELL)
            high, low = halves(moment_ref[pl.ds(start, PER_CELL), :])
            parts.append(dims(high, atoms, 0, 0) + dims(low, atoms, 0, 0))
        back = jnp.concatenate(parts, 1)
        weighted = basis * weight
        grad_weighted = jnp.zeros((NBASIS, PAIRS), F32)
        for m in range(9):
            block = back[m * NBASIS : (m + 1) * NBASIS]
            grad_weighted += block * harmonic[m : m + 1]
            chain_ref[i, m : m + 1, :] = grad_ref[i, G_Y + m : G_Y + m + 1, :] + jnp.sum(
                block * weighted, 0, keepdims=True
            )
        grad_basis = grad_ref[i, G_B : G_B + NBASIS, :] + grad_weighted * weight
        grad_weight = grad_ref[i, G_E : G_E + 1, :] + jnp.sum(
            grad_weighted * basis, 0, keepdims=True
        )
        chain_ref[i, 9:10, :] = (
            jnp.sum(grad_basis * slope, 0, keepdims=True) + grad_weight * weight_slope
        )
        return carry

    lax.fori_loop(0, COLS, column, 0)

    def chain(row):
        return chain_ref[:, row, :]

    def feature(row):
        return whole_feature(feat_ref, row)

    three, five, fifteen = math.sqrt(3.0), math.sqrt(5.0), math.sqrt(15.0)
    nx, ny, nz = (feature(F_Y + 1 + c) * (1.0 / three) for c in range(3))
    grad_x = three * chain(1) + fifteen * (ny * chain(4) + nz * chain(7) + nx * chain(8))
    grad_y = three * chain(2) + fifteen * (nx * chain(4) + nz * chain(5) - ny * chain(8))
    grad_z = (
        three * chain(3) + fifteen * (ny * chain(5) + nx * chain(7)) + (3.0 * five) * nz * chain(6)
    )
    inverse = feature(F_INV)
    along = chain(9) - inverse * (nx * grad_x + ny * grad_y + nz * grad_z)
    pull_ref[0] = grad_x * inverse + nx * along
    pull_ref[1] = grad_y * inverse + ny * along
    pull_ref[2] = grad_z * inverse + nz * along

    gather = one_hot(iota((32, PAIRS), 0) == (iota((32, PAIRS), 1) >> 5))
    for c in range(3):
        high, low = halves(pull_ref[c])
        own_ref[c] = dims(high, gather, 1, 1) + dims(low, gather, 1, 1)

    row_cells = iota((5 * CELL_ROWS, PAIRS), 0)
    row_slots = iota((PER_CELL, PAIRS), 0)
    ghost_ref[...] = jnp.zeros_like(ghost_ref)

    def scatter(i, carry):
        x, y = i // CY, i % CY
        hot = one_hot(row_cells == code_ref[2, pl.ds(i, 1), :])
        mask = row_slots == code_ref[3, pl.ds(i, 1), :]
        kept = jnp.concatenate(
            [jnp.where(mask, pull_ref[c, pl.ds(i, 1), :], 0.0) for c in range(3)], 0
        )
        high, low = halves(kept)
        found = dims(hot, high, 1, 1) + dims(hot, low, 1, 1)
        for dx in range(5):
            start = pl.multiple_of(((x + dx) * 8 + y) * 8, 8)
            ghost_ref[pl.ds(start, CELL_ROWS), :] += found[dx * CELL_ROWS : (dx + 1) * CELL_ROWS]
        return carry

    lax.fori_loop(0, COLS, scatter, 0)


def call(kernel, outs, scratch, *args):
    return pl.pallas_call(
        kernel,
        out_shape=[jax.ShapeDtypeStruct(shape, dtype) for shape, dtype in outs],
        scratch_shapes=[pltpu.VMEM(shape, dtype) for shape, dtype in scratch],
        compiler_params=pltpu.CompilerParams(vmem_limit_bytes=56 * 2**20),
    )(*args)


def shifted(block, axis, distance):
    size = lax.axis_size(axis)
    return lax.ppermute(block, axis, [(i, (i + distance) % size) for i in range(size)])


def padded(array, axis, dim, tail=0):
    length = array.shape[dim]
    before = shifted(lax.slice_in_dim(array, length - 2, length, axis=dim), axis, 1)
    after = shifted(lax.slice_in_dim(array, 0, 2, axis=dim), axis, -1)
    parts = [before, array, after]
    if tail:
        parts.append(jnp.zeros(after.shape[:dim] + (tail,) + after.shape[dim + 1 :], array.dtype))
    return jnp.concatenate(parts, axis=dim)


def folded(array, axis, dim, length):
    lower = lax.slice_in_dim(array, 0, 2, axis=dim).astype(BF16)
    upper = lax.slice_in_dim(array, length + 2, length + 4, axis=dim).astype(BF16)
    core = lax.slice_in_dim(array, 2, length + 2, axis=dim).astype(F32)
    to_first = shifted(upper, axis, 1).astype(F32)
    to_last = shifted(lower, axis, -1).astype(F32)
    if length == 2:
        return core + to_first + to_last
    first = lax.slice_in_dim(core, 0, 2, axis=dim) + to_first
    last = lax.slice_in_dim(core, 2, 4, axis=dim) + to_last
    return jnp.concatenate([first, last], axis=dim)


def shards(
    offsets,
    species,
    neighbours,
    counts,
    embed,
    radial_a,
    mix_in,
    proj_center,
    proj_neigh,
    radial_b,
    couple,
    latent_two,
    latent_three,
    readout,
):
    numbers = neighbours.reshape(COLS, PAIRS)
    places = offsets.reshape(CX, CY, CZ, 48)
    around = padded(padded(padded(places, "gx", 0), "gy", 1), "gz", 2, tail=2)
    own = offsets.reshape(COLS, CZ, 3, PER_CELL).transpose(2, 0, 1, 3).reshape(3 * COLS, 32)
    hidden, env, scale, feats, codes = call(
        env_kernel,
        [
            ((ATOMS, CH), BF16),
            ((9, ATOMS, CH), F32),
            ((ATOMS, CH), F32),
            ((PAIRS // 128 * F_COUNT * COLS, 128), F32),
            ((4, COLS, PAIRS), jnp.int32),
        ],
        [((3, COLS, PAIRS), F32), ((ATOMS, 72), F32)],
        numbers,
        around.reshape(512, 48),
        own,
        counts.reshape(COLS, 32),
        species.reshape(1, ATOMS),
        embed,
        radial_a,
        mix_in,
    )
    grid = hidden.reshape(CX, CY, CZ, PER_CELL, CH)
    wide = padded(padded(padded(grid, "gx", 0), "gy", 1), "gz", 2)
    energy, ghost, grad_center, grad_env, grads = call(
        pair_kernel,
        [
            ((COLS, 32), F32),
            ((64, 2, RUN, CH), BF16),
            ((ATOMS, CH), F32),
            ((9, ATOMS, CH), F32),
            ((COLS, G_COUNT, PAIRS), F32),
        ],
        [
            ((64 * RUN, 2 * CH), BF16),
            ((64 * RUN, 2 * CH), F32),
            ((5 * SLAB, PAIRS), BF16),
            ((ATOMS, CH), F32),
            ((COLS, PAIRS), F32),
        ],
        wide.reshape(64, 2, RUN, CH),
        hidden,
        env,
        feats,
        codes,
        proj_center,
        proj_neigh,
        radial_b,
        couple,
        latent_two,
        latent_three,
        readout.reshape(1, CH),
    )
    ghost = ghost.reshape(CX + 4, CY + 4, CZ + 4, PER_CELL, CH)
    owned = folded(folded(folded(ghost, "gx", 0, CX), "gy", 1, CY), "gz", 2, CZ)
    own_pull, far_pull = call(
        force_kernel,
        [((3, COLS, 32), F32), ((512, 48), F32)],
        [((ATOMS, 72), F32), ((COLS, 16, PAIRS), F32), ((3, COLS, PAIRS), F32)],
        owned.reshape(ATOMS, CH),
        grad_center,
        grad_env,
        env,
        scale,
        feats,
        codes,
        grads,
        mix_in,
        proj_center,
        proj_neigh,
        radial_a,
        couple,
    )
    far = far_pull.reshape(CX + 4, CY + 4, 8, 48)
    far = folded(folded(folded(far, "gx", 0, CX), "gy", 1, CY), "gz", 2, CZ)
    near = own_pull.reshape(3, CX, CY, CZ, PER_CELL).transpose(1, 2, 3, 0, 4)
    forces = near - far.reshape(CX, CY, CZ, 3, PER_CELL)
    return (forces, energy.reshape(CX, CY, CZ, PER_CELL))


def solution(mesh):
    placed = (
        P("gx", "gy", "gz", None, None),
        P("gx", "gy", "gz", None),
        P("gx", "gy", "gz", None, None),
        P("gx", "gy", "gz", None),
    ) + (P(),) * 10
    return jax.shard_map(
        shards,
        mesh=mesh,
        in_specs=placed,
        out_specs=(P("gx", "gy", "gz", None, None), P("gx", "gy", "gz", None)),
        check_vma=False,
    )
```

time: 1900 us -> 210 us (0.11)
  local copies, waits for them, and re-layouts: 826 us -> 12.9 us
  other arithmetic: 485 us -> 6.66 us
  matrix products: 430 us -> 0 us
  Pallas kernels: 0 us -> 89.5 us
  loops' own time: 41.8 us -> 0 us
    dot_general x100 -> x0, matrix products: 430 us -> none  [the longest x16 107 us: layer_energy(): jnp.einsum('mak,mac->akc', harmonic_values, environment * couple_full[:,...]
    gather x40 -> x0, local copies, waits for them, and re-layouts: 366 us -> none  [the longest x16 227 us: layer_geometry(): other_place = flat_offsets[layer_nbr]]
    scatter-add x20 -> x0, other arithmetic: 315 us -> none  [the longest x8 196 us: layer_geometry(): other_place = flat_offsets[layer_nbr]]
    while x432 -> x0, local copies, waits for them, and re-layouts: 148 us -> none
    slice x56 -> x16, local copies, waits for them, and re-layouts: 121 us -> 4.26 us  [the longest x4 1.32 us: folded(): lower = lax.slice_in_dim(array, 0, 2, axis=dim).astype(BF16)]
    pallas_call x0 -> x3, Pallas kernels: none -> 89.5 us  [call(): pl.pallas_call(kernel, out_shape=[jax.ShapeDtypeStruct(shape, dtype) for...]
    add_any x28 -> x0, other arithmetic: 49.4 us -> none  [the longest x4 22.6 us: brick_energy(): lax.map(jax.checkpoint(one_layer), (jnp.arange(CX, dtype=jnp.int32), nbr_...]
    another operation x4 -> x0, loops' own time: 41.8 us -> none  [the longest x2 32.9 us: brick_energy(): lax.map(jax.checkpoint(one_layer), (jnp.arange(CX, dtype=jnp.int32), nbr_...]
  transfers between devices with their start and end apart: 24 -> 24, of which waited for: 19 -> 18; matrix products, arithmetic and copies ran while one was open for 18% -> 4% of each run, Pallas kernels for 0% -> 0%
where the time goes in v1:
time: 210 us; the launch traced here: 206 us
  Pallas kernels  89.5 us (43%)
  waiting for transfers between devices  55.7 us (27%)
  starting transfers between devices  40.6 us (19%)
  local copies, waits for them, and re-layouts  12.9 us (6%)
  other arithmetic  6.66 us (3%)
    pallas_call x3, Pallas kernels, call(): pl.pallas_call(kernel, out_shape=[jax.ShapeDtypeStruct(shape, dtype) for...  89.5 us
    ppermute x24, waiting for transfers between devices, shifted(): lax.ppermute(block, axis, [(i, (i + distance) % size) for i in range(size)])  55.7 us
    ppermute x24, starting transfers between devices, shifted(): lax.ppermute(block, axis, [(i, (i + distance) % size) for i in range(size)])  40.6 us
  transfers between devices with their start and end apart: 24, of which 18 were waited for; matrix products, arithmetic and copies ran while one was open for 4% of the time, Pallas kernels for 0%

profile of v1, /device:TPU:6, one launch (start us, length us, event | category | flops | bytes accessed | tf_op | source)
XLA Modules:
  0.0 206.4 jit_solution(9125128778693174963)
XLA Ops:
  0.6 0.8 fusion.27
  1.7 3.4 %collective-permute-start.1 = (f32[2,4,2,48]{3,2,1,0:T(2,128)S(1)}, f32[2,4,2,48]{3,2,1,0:T(2,128)S(1)}, u32[]{:S(2)}, u32[]{:S(2)}) collective-permute-start(f32[2,4,2,48]{3,2,1,0:T(2,128)S(1)} %slice.149), channel_id=1, source_target_pairs={{0,96},{32,0},{64,32},{96,64},{1,97},{33,1},{65,33},{97,65},{2,98}... | collective-permute-start | bytes 9224 | tf_op jit(solution)/shard_map/ppermute | solution.py:540
  5.1 0.8 copy.19
  7.0 1.5 collective-permute-start.3
  8.5 1.7 collective-permute-done.2
  10.3 1.7 collective-permute-done.3
  12.0 4.3 %collective-permute-start.5 = (f32[8,8,2,48]{3,2,1,0:T(2,128)S(1)}, f32[8,8,2,48]{3,2,1,0:T(2,128)S(1)}, u32[]{:S(2)}, u32[]{:S(2)}) collective-permute-start(f32[8,8,2,48]{3,2,1,0:T(2,128)S(1)} %pad_maximum_fusion.7), channel_id=1, source_target_pairs={{0,7},{1,0},{2,1},{3,2},{4,3},{5,4},{6,5},{7,6},{8,15},{9,8},{10,9... | collective-permute-start | bytes 73736 | tf_op jit(solution)/shard_map/ppermute | solution.py:540
  16.3 0.8 copy_bitcast_fusion
  17.2 1.4 reshape.71.species_ref
  18.6 1.4 reshape.70.count_ref
  20.0 0.7 reshape.69.own_ref
  20.7 1.7 reshape.65.nbr_ref
  23.1 0.9 maximum_maximum_fusion
  24.0 14.0 %shard_map.149 = (bf16[512,128]{1,0:T(8,128)(2,1)}, f32[9,512,128]{2,1,0:T(8,128)}, f32[512,128]{1,0:T(8,128)}, f32[3584,128]{1,0:T(8,128)}, s32[4,16,1024]{2,1,0:T(8,128)}) custom-call(s32[16,1024]{1,0:T(8,128)} %reshape.65.nbr_ref, f32[512,48]{1,0:T(8,128)} %bitcast.31, f32[48,32]{1,0:T(8,128)} %reshape.69.own_ref, s32[16,32]{1,0:T(8,128)} %reshape.70.count_ref, ...), custom_call_target="tpu_custom_call" | custom-call | tf_op jit(solution)/shard_map/pallas_call | solution.py:530
  38.0 0.9 fusion.25
  38.9 1.5 collective-permute-start.7
  40.4 1.9 collective-permute-done.7
  42.3 3.4 %collective-permute-done.6 = bf16[2,4,2,16,128]{4,3,2,1,0:T(8,128)(2,1)S(1)} collective-permute-done((bf16[2,4,2,16,128]{4,3,2,1,0:T(8,128)(2,1)S(1)}, bf16[2,4,2,16,128]{4,3,2,1,0:T(8,128)(2,1)S(1)}, u32[]{:S(2)}, u32[]{:S(2)}) %collective-permute-start.6) | collective-permute-done | bytes 65568 | tf_op jit(solution)/shard_map/ppermute | solution.py:540
  45.7 0.9 pad_maximum_fusion.4
  47.2 1.6 collective-permute-start.9
  48.8 3.0 %collective-permute-done.8 = bf16[8,2,2,16,128]{4,3,2,1,0:T(8,128)(2,1)S(1)} collective-permute-done((bf16[8,2,2,16,128]{4,3,2,1,0:T(8,128)(2,1)S(1)}, bf16[8,2,2,16,128]{4,3,2,1,0:T(8,128)(2,1)S(1)}, u32[]{:S(2)}, u32[]{:S(2)}) %collective-permute-start.8) | collective-permute-done | bytes 131104 | tf_op jit(solution)/shard_map/ppermute | solution.py:540
  51.8 1.6 collective-permute-done.9
  53.4 1.0 pad_maximum_fusion.3
  54.4 4.1 %collective-permute-start.11 = (bf16[8,8,2,16,128]{4,3,2,1,0:T(8,128)(2,1)S(1)}, bf16[8,8,2,16,128]{4,3,2,1,0:T(8,128)(2,1)S(1)}, u32[]{:S(2)}, u32[]{:S(2)}) collective-permute-start(bf16[8,8,2,16,128]{4,3,2,1,0:T(8,128)(2,1)S(1)} %pad_maximum_fusion.3), channel_id=1, source_target_pairs={{0,7},{1,0},{2,1},{3,2},{4,3},{5,4},{6,5},{7,6},{8,15},{9,8},{10,9... | collective-permute-start | bytes 1572872 | tf_op jit(solution)/shard_map/ppermute | solution.py:540
  58.4 19.2 %collective-permute-done.11 = bf16[8,8,2,16,128]{4,3,2,1,0:T(8,128)(2,1)S(1)} collective-permute-done((bf16[8,8,2,16,128]{4,3,2,1,0:T(8,128)(2,1)S(1)}, bf16[8,8,2,16,128]{4,3,2,1,0:T(8,128)(2,1)S(1)}, u32[]{:S(2)}, u32[]{:S(2)}) %collective-permute-start.11) | collective-permute-done | bytes 524320 | tf_op jit(solution)/shard_map/ppermute | solution.py:540
  77.6 1.4 pad_maximum_fusion.1
  79.0 56.2 %shard_map.150 = (f32[16,32]{1,0:T(8,128)}, bf16[64,2,48,128]{3,2,1,0:T(8,128)(2,1)}, f32[512,128]{1,0:T(8,128)}, f32[9,512,128]{2,1,0:T(8,128)}, f32[16,24,1024]{2,1,0:T(8,128)}) custom-call(bf16[64,2,48,128]{3,2,1,0:T(8,128)(2,1)} %bitcast.24, bf16[512,128]{1,0:T(8,128)(2,1)} %get-tuple-element.14.hidden_ref, f32[9,512,128]{2,1,0:T(8,128)} %get-tuple-element.15.env_ref, ...), custom_call_target="tpu_custom_call" | custom-call | tf_op jit(solution)/shard_map/pallas_call | solution.py:530
  135.2 1.3 fusion.18
  137.0 3.2 %collective-permute-start.13 = (bf16[2,8,6,16,128]{4,3,2,1,0:T(8,128)(2,1)S(1)}, bf16[2,8,6,16,128]{4,3,2,1,0:T(8,128)(2,1)S(1)}, u32[]{:S(2)}, u32[]{:S(2)}) collective-permute-start(bf16[2,8,6,16,128]{4,3,2,1,0:T(8,128)(2,1)S(1)} %bitcast.32), channel_id=1, source_target_pairs={{0,96},{32,0},{64,32},{96,64},{1,97},{33,1},{65,33},{97,65},{2,98}... | collective-permute-start | bytes 1179656 | tf_op jit(solution)/shard_map/ppermute | solution.py:540
  140.4 7.8 %collective-permute-done.12 = bf16[2,8,6,16,128]{4,3,2,1,0:T(8,128)(2,1)S(1)} collective-permute-done((bf16[2,8,6,16,128]{4,3,2,1,0:T(8,128)(2,1)S(1)}, bf16[2,8,6,16,128]{4,3,2,1,0:T(8,128)(2,1)S(1)}, u32[]{:S(2)}, u32[]{:S(2)}) %collective-permute-start.12) | collective-permute-done | bytes 393248 | tf_op jit(solution)/shard_map/ppermute | solution.py:540
  148.5 1.4 collective-permute-start.15
  149.9 1.9 collective-permute-start.14
  151.8 5.5 %collective-permute-done.15 = bf16[4,2,6,16,128]{4,3,2,1,0:T(8,128)(2,1)S(1)} collective-permute-done((bf16[4,2,6,16,128]{4,3,2,1,0:T(8,128)(2,1)S(1)}, bf16[4,2,6,16,128]{4,3,2,1,0:T(8,128)(2,1)S(1)}, u32[]{:S(2)}, u32[]{:S(2)}) %collective-permute-start.15) | collective-permute-done | bytes 196640 | tf_op jit(solution)/shard_map/ppermute | solution.py:540
  157.5 2.7 %collective-permute-start.16 = (bf16[4,4,2,16,128]{4,3,2,1,0:T(8,128)(2,1)S(1)}, bf16[4,4,2,16,128]{4,3,2,1,0:T(8,128)(2,1)S(1)}, u32[]{:S(2)}, u32[]{:S(2)}) collective-permute-start(bf16[4,4,2,16,128]{4,3,2,1,0:T(8,128)(2,1)S(1)} %get-tuple-element.36), channel_id=1, source_target_pairs={{0,1},{1,2},{2,3},{3,4},{4,5},{5,6},{6,7},{7,0},{8,9},{9,10},{10,1... | collective-permute-start | bytes 393224 | tf_op jit(solution)/shard_map/ppermute | solution.py:540
  160.2 2.7 %collective-permute-start.17 = (bf16[4,4,2,16,128]{4,3,2,1,0:T(8,128)(2,1)S(1)}, bf16[4,4,2,16,128]{4,3,2,1,0:T(8,128)(2,1)S(1)}, u32[]{:S(2)}, u32[]{:S(2)}) collective-permute-start(bf16[4,4,2,16,128]{4,3,2,1,0:T(8,128)(2,1)S(1)} %get-tuple-element.37), channel_id=1, source_target_pairs={{0,7},{1,0},{2,1},{3,2},{4,3},{5,4},{6,5},{7,6},{8,15},{9,8},{10,9... | collective-permute-start | bytes 393224 | tf_op jit(solution)/shard_map/ppermute | solution.py:540
  163.0 2.9 %collective-permute-done.16 = bf16[4,4,2,16,128]{4,3,2,1,0:T(8,128)(2,1)S(1)} collective-permute-done((bf16[4,4,2,16,128]{4,3,2,1,0:T(8,128)(2,1)S(1)}, bf16[4,4,2,16,128]{4,3,2,1,0:T(8,128)(2,1)S(1)}, u32[]{:S(2)}, u32[]{:S(2)}) %collective-permute-start.16) | collective-permute-done | bytes 131104 | tf_op jit(solution)/shard_map/ppermute | solution.py:540
  165.9 1.6 collective-permute-done.17
  167.5 0.8 fusion.8
  168.3 19.3 %shard_map.151 = (f32[3,16,32]{2,1,0:T(8,128)}, f32[512,48]{1,0:T(8,128)}) custom-call(f32[512,128]{1,0:T(8,128)} %bitcast.30, f32[512,128]{1,0:T(8,128)} %get-tuple-element.19.grad_center_ref, f32[9,512,128]{2,1,0:T(8,128)} %get-tuple-element.20.grad_env_ref, f32[9,512,128]{2,1,0:T(8,128)} %get-tuple-element.15.env_ref, ...), custom_call_target="tpu_custom_call" | custom-call | tf_op jit(solution)/shard_map/pallas_call | solution.py:530
  187.6 1.0 convert.22
  188.7 0.9 fusion.22
  189.6 3.3 %collective-permute-start.19 = (bf16[2,8,8,48]{3,2,1,0:T(8,128)(2,1)S(1)}, bf16[2,8,8,48]{3,2,1,0:T(8,128)(2,1)S(1)}, u32[]{:S(2)}, u32[]{:S(2)}) collective-permute-start(bf16[2,8,8,48]{3,2,1,0:T(8,128)(2,1)S(1)} %bitcast.38), channel_id=1, source_target_pairs={{0,96},{32,0},{64,32},{96,64},{1,97},{33,1},{65,33},{97,65},{2,98}... | collective-permute-start | bytes 36872 | tf_op jit(solution)/shard_map/ppermute | solution.py:540
  193.6 0.9 collective-permute-done.19
  194.6 3.2 %collective-permute-start.20 = (bf16[4,2,8,48]{3,2,1,0:T(8,128)(2,1)S(1)}, bf16[4,2,8,48]{3,2,1,0:T(8,128)(2,1)S(1)}, u32[]{:S(2)}, u32[]{:S(2)}) collective-permute-start(bf16[4,2,8,48]{3,2,1,0:T(8,128)(2,1)S(1)} %get-tuple-element.49), channel_id=1, source_target_pairs={{0,8},{8,16},{16,24},{24,0},{1,9},{9,17},{17,25},{25,1},{2,10},{10... | collective-permute-start | bytes 18440 | tf_op jit(solution)/shard_map/ppermute | solution.py:540
  197.9 1.8 collective-permute-done.21
  200.0 4.0 %collective-permute-start.23 = (bf16[4,4,2,48]{3,2,1,0:T(2,128)(2,1)S(1)}, bf16[4,4,2,48]{3,2,1,0:T(2,128)(2,1)S(1)}, u32[]{:S(2)}, u32[]{:S(2)}) collective-permute-start(bf16[4,4,2,48]{3,2,1,0:T(2,128)(2,1)S(1)} %get-tuple-element.53), channel_id=1, source_target_pairs={{0,7},{1,0},{2,1},{3,2},{4,3},{5,4},{6,5},{7,6},{8,15},{9,8},{10,9... | collective-permute-start | bytes 9224 | tf_op jit(solution)/shard_map/ppermute | solution.py:540
  204.0 0.7 reshape.78
  204.8 0.8 collective-permute-done.22
  (63 shorter events, 5.8 us)
Async XLA Ops:
  1.5 4.7 %collective-permute-start = (f32[2,4,2,48]{3,2,1,0:T(2,128)S(1)}, f32[2,4,2,48]{3,2,1,0:T(2,128)S(1)}, u32[]{:S(2)}, u32[]{:S(2)}) collective-permute-start(f32[2,4,2,48]{3,2,1,0:T(2,128)S(1)} %slice.147), channel_id=1, source_target_pairs={{0,32},{32,64},{64,96},{96,0},{1,33},{33,65},{65,97},{97,1},{2,34}... | collective-permute-start | bytes 9224 | tf_op jit(solution)/shard_map/ppermute | solution.py:540
  1.7 4.7 %collective-permute-start.1 = (f32[2,4,2,48]{3,2,1,0:T(2,128)S(1)}, f32[2,4,2,48]{3,2,1,0:T(2,128)S(1)}, u32[]{:S(2)}, u32[]{:S(2)}) collective-permute-start(f32[2,4,2,48]{3,2,1,0:T(2,128)S(1)} %slice.149), channel_id=1, source_target_pairs={{0,96},{32,0},{64,32},{96,64},{1,97},{33,1},{65,33},{97,65},{2,98}... | collective-permute-start | bytes 9224 | tf_op jit(solution)/shard_map/ppermute | solution.py:540
  6.5 3.8 %collective-permute-start.2 = (f32[8,2,2,48]{3,2,1,0:T(2,128)S(1)}, f32[8,2,2,48]{3,2,1,0:T(2,128)S(1)}, u32[]{:S(2)}, u32[]{:S(2)}) collective-permute-start(f32[8,2,2,48]{3,2,1,0:T(2,128)S(1)} %get-tuple-element.54), channel_id=1, source_target_pairs={{0,8},{8,16},{16,24},{24,0},{1,9},{9,17},{17,25},{25,1},{2,10},{10... | collective-permute-start | bytes 18440 | tf_op jit(solution)/shard_map/ppermute | solution.py:540
  7.0 4.9 %collective-permute-start.3 = (f32[8,2,2,48]{3,2,1,0:T(2,128)S(1)}, f32[8,2,2,48]{3,2,1,0:T(2,128)S(1)}, u32[]{:S(2)}, u32[]{:S(2)}) collective-permute-start(f32[8,2,2,48]{3,2,1,0:T(2,128)S(1)} %get-tuple-element.55), channel_id=1, source_target_pairs={{0,24},{8,0},{16,8},{24,16},{1,25},{9,1},{17,9},{25,17},{2,26},{10... | collective-permute-start | bytes 18440 | tf_op jit(solution)/shard_map/ppermute | solution.py:540
  12.0 10.5 %collective-permute-start.5 = (f32[8,8,2,48]{3,2,1,0:T(2,128)S(1)}, f32[8,8,2,48]{3,2,1,0:T(2,128)S(1)}, u32[]{:S(2)}, u32[]{:S(2)}) collective-permute-start(f32[8,8,2,48]{3,2,1,0:T(2,128)S(1)} %pad_maximum_fusion.7), channel_id=1, source_target_pairs={{0,7},{1,0},{2,1},{3,2},{4,3},{5,4},{6,5},{7,6},{8,15},{9,8},{10,9... | collective-permute-start | bytes 73736 | tf_op jit(solution)/shard_map/ppermute | solution.py:540
  16.3 6.8 %collective-permute-start.4 = (f32[8,8,2,48]{3,2,1,0:T(2,128)S(1)}, f32[8,8,2,48]{3,2,1,0:T(2,128)S(1)}, u32[]{:S(2)}, u32[]{:S(2)}) collective-permute-start(f32[8,8,2,48]{3,2,1,0:T(2,128)S(1)} %pad_maximum_fusion.7), channel_id=1, source_target_pairs={{0,1},{1,2},{2,3},{3,4},{4,5},{5,6},{6,7},{7,0},{8,9},{9,10},{10,1... | collective-permute-start | bytes 73736 | tf_op jit(solution)/shard_map/ppermute | solution.py:540
  38.0 39.6 %copy-start = (bf16[512,128]{1,0:T(8,128)(2,1)S(1)}, bf16[512,128]{1,0:T(8,128)(2,1)}, u32[]{:S(2)}) copy-start(bf16[512,128]{1,0:T(8,128)(2,1)} %get-tuple-element.14.hidden_ref) | copy-start | bytes 393220
  38.9 3.4 %collective-permute-start.7 = (bf16[2,4,2,16,128]{4,3,2,1,0:T(8,128)(2,1)S(1)}, bf16[2,4,2,16,128]{4,3,2,1,0:T(8,128)(2,1)S(1)}, u32[]{:S(2)}, u32[]{:S(2)}) collective-permute-start(bf16[2,4,2,16,128]{4,3,2,1,0:T(8,128)(2,1)S(1)} %bitcast.37), channel_id=1, source_target_pairs={{0,96},{32,0},{64,32},{96,64},{1,97},{33,1},{65,33},{97,65},{2,98}... | collective-permute-start | bytes 196616 | tf_op jit(solution)/shard_map/ppermute | solution.py:540
  40.4 5.3 %collective-permute-start.6 = (bf16[2,4,2,16,128]{4,3,2,1,0:T(8,128)(2,1)S(1)}, bf16[2,4,2,16,128]{4,3,2,1,0:T(8,128)(2,1)S(1)}, u32[]{:S(2)}, u32[]{:S(2)}) collective-permute-start(bf16[2,4,2,16,128]{4,3,2,1,0:T(8,128)(2,1)S(1)} %bitcast.36), channel_id=1, source_target_pairs={{0,32},{32,64},{64,96},{96,0},{1,33},{33,65},{65,97},{97,1},{2,34}... | collective-permute-start | bytes 196616 | tf_op jit(solution)/shard_map/ppermute | solution.py:540
  46.7 5.1 %collective-permute-start.8 = (bf16[8,2,2,16,128]{4,3,2,1,0:T(8,128)(2,1)S(1)}, bf16[8,2,2,16,128]{4,3,2,1,0:T(8,128)(2,1)S(1)}, u32[]{:S(2)}, u32[]{:S(2)}) collective-permute-start(bf16[8,2,2,16,128]{4,3,2,1,0:T(8,128)(2,1)S(1)} %get-tuple-element.40), channel_id=1, source_target_pairs={{0,8},{8,16},{16,24},{24,0},{1,9},{9,17},{17,25},{25,1},{2,10},{10... | collective-permute-start | bytes 393224 | tf_op jit(solution)/shard_map/ppermute | solution.py:540
  47.2 6.2 %collective-permute-start.9 = (bf16[8,2,2,16,128]{4,3,2,1,0:T(8,128)(2,1)S(1)}, bf16[8,2,2,16,128]{4,3,2,1,0:T(8,128)(2,1)S(1)}, u32[]{:S(2)}, u32[]{:S(2)}) collective-permute-start(bf16[8,2,2,16,128]{4,3,2,1,0:T(8,128)(2,1)S(1)} %get-tuple-element.41), channel_id=1, source_target_pairs={{0,24},{8,0},{16,8},{24,16},{1,25},{9,1},{17,9},{25,17},{2,26},{10... | collective-permute-start | bytes 393224 | tf_op jit(solution)/shard_map/ppermute | solution.py:540
  54.4 23.2 %collective-permute-start.11 = (bf16[8,8,2,16,128]{4,3,2,1,0:T(8,128)(2,1)S(1)}, bf16[8,8,2,16,128]{4,3,2,1,0:T(8,128)(2,1)S(1)}, u32[]{:S(2)}, u32[]{:S(2)}) collective-permute-start(bf16[8,8,2,16,128]{4,3,2,1,0:T(8,128)(2,1)S(1)} %pad_maximum_fusion.3), channel_id=1, source_target_pairs={{0,7},{1,0},{2,1},{3,2},{4,3},{5,4},{6,5},{7,6},{8,15},{9,8},{10,9... | collective-permute-start | bytes 1572872 | tf_op jit(solution)/shard_map/ppermute | solution.py:540
  58.4 19.2 %collective-permute-start.10 = (bf16[8,8,2,16,128]{4,3,2,1,0:T(8,128)(2,1)S(1)}, bf16[8,8,2,16,128]{4,3,2,1,0:T(8,128)(2,1)S(1)}, u32[]{:S(2)}, u32[]{:S(2)}) collective-permute-start(bf16[8,8,2,16,128]{4,3,2,1,0:T(8,128)(2,1)S(1)} %pad_maximum_fusion.3), channel_id=1, source_target_pairs={{0,1},{1,2},{2,3},{3,4},{4,5},{5,6},{6,7},{7,0},{8,9},{9,10},{10,1... | collective-permute-start | bytes 1572872 | tf_op jit(solution)/shard_map/ppermute | solution.py:540
  135.2 1.6 copy-start.1
  136.5 11.7 %collective-permute-start.12 = (bf16[2,8,6,16,128]{4,3,2,1,0:T(8,128)(2,1)S(1)}, bf16[2,8,6,16,128]{4,3,2,1,0:T(8,128)(2,1)S(1)}, u32[]{:S(2)}, u32[]{:S(2)}) collective-permute-start(bf16[2,8,6,16,128]{4,3,2,1,0:T(8,128)(2,1)S(1)} %bitcast.33), channel_id=1, source_target_pairs={{0,32},{32,64},{64,96},{96,0},{1,33},{33,65},{65,97},{97,1},{2,34}... | collective-permute-start | bytes 1179656 | tf_op jit(solution)/shard_map/ppermute | solution.py:540
  137.0 11.2 %collective-permute-start.13 = (bf16[2,8,6,16,128]{4,3,2,1,0:T(8,128)(2,1)S(1)}, bf16[2,8,6,16,128]{4,3,2,1,0:T(8,128)(2,1)S(1)}, u32[]{:S(2)}, u32[]{:S(2)}) collective-permute-start(bf16[2,8,6,16,128]{4,3,2,1,0:T(8,128)(2,1)S(1)} %bitcast.32), channel_id=1, source_target_pairs={{0,96},{32,0},{64,32},{96,64},{1,97},{33,1},{65,33},{97,65},{2,98}... | collective-permute-start | bytes 1179656 | tf_op jit(solution)/shard_map/ppermute | solution.py:540
  148.5 8.8 %collective-permute-start.15 = (bf16[4,2,6,16,128]{4,3,2,1,0:T(8,128)(2,1)S(1)}, bf16[4,2,6,16,128]{4,3,2,1,0:T(8,128)(2,1)S(1)}, u32[]{:S(2)}, u32[]{:S(2)}) collective-permute-start(bf16[4,2,6,16,128]{4,3,2,1,0:T(8,128)(2,1)S(1)} %get-tuple-element.34), channel_id=1, source_target_pairs={{0,24},{8,0},{16,8},{24,16},{1,25},{9,1},{17,9},{25,17},{2,26},{10... | collective-permute-start | bytes 589832 | tf_op jit(solution)/shard_map/ppermute | solution.py:540
  149.9 7.5 %collective-permute-start.14 = (bf16[4,2,6,16,128]{4,3,2,1,0:T(8,128)(2,1)S(1)}, bf16[4,2,6,16,128]{4,3,2,1,0:T(8,128)(2,1)S(1)}, u32[]{:S(2)}, u32[]{:S(2)}) collective-permute-start(bf16[4,2,6,16,128]{4,3,2,1,0:T(8,128)(2,1)S(1)} %get-tuple-element.35), channel_id=1, source_target_pairs={{0,8},{8,16},{16,24},{24,0},{1,9},{9,17},{17,25},{25,1},{2,10},{10... | collective-permute-start | bytes 589832 | tf_op jit(solution)/shard_map/ppermute | solution.py:540
  157.5 8.3 %collective-permute-start.16 = (bf16[4,4,2,16,128]{4,3,2,1,0:T(8,128)(2,1)S(1)}, bf16[4,4,2,16,128]{4,3,2,1,0:T(8,128)(2,1)S(1)}, u32[]{:S(2)}, u32[]{:S(2)}) collective-permute-start(bf16[4,4,2,16,128]{4,3,2,1,0:T(8,128)(2,1)S(1)} %get-tuple-element.36), channel_id=1, source_target_pairs={{0,1},{1,2},{2,3},{3,4},{4,5},{5,6},{6,7},{7,0},{8,9},{9,10},{10,1... | collective-permute-start | bytes 393224 | tf_op jit(solution)/shard_map/ppermute | solution.py:540
  160.2 7.3 %collective-permute-start.17 = (bf16[4,4,2,16,128]{4,3,2,1,0:T(8,128)(2,1)S(1)}, bf16[4,4,2,16,128]{4,3,2,1,0:T(8,128)(2,1)S(1)}, u32[]{:S(2)}, u32[]{:S(2)}) collective-permute-start(bf16[4,4,2,16,128]{4,3,2,1,0:T(8,128)(2,1)S(1)} %get-tuple-element.37), channel_id=1, source_target_pairs={{0,7},{1,0},{2,1},{3,2},{4,3},{5,4},{6,5},{7,6},{8,15},{9,8},{10,9... | collective-permute-start | bytes 393224 | tf_op jit(solution)/shard_map/ppermute | solution.py:540
  187.6 16.3 %copy-start.3 = (f32[16,32]{1,0:T(8,128)S(1)}, f32[16,32]{1,0:T(8,128)}, u32[]{:S(2)}) copy-start(f32[16,32]{1,0:T(8,128)} %get-tuple-element.25) | copy-start | bytes 6148
  187.6 17.0 %copy-start.2 = (f32[3,16,32]{2,1,0:T(8,128)S(1)}, f32[3,16,32]{2,1,0:T(8,128)}, u32[]{:S(2)}) copy-start(f32[3,16,32]{2,1,0:T(8,128)} %get-tuple-element.23) | copy-start | bytes 18436
  188.7 4.9 %collective-permute-start.18 = (bf16[2,8,8,48]{3,2,1,0:T(8,128)(2,1)S(1)}, bf16[2,8,8,48]{3,2,1,0:T(8,128)(2,1)S(1)}, u32[]{:S(2)}, u32[]{:S(2)}) collective-permute-start(bf16[2,8,8,48]{3,2,1,0:T(8,128)(2,1)S(1)} %bitcast.39), channel_id=1, source_target_pairs={{0,32},{32,64},{64,96},{96,0},{1,33},{33,65},{65,97},{97,1},{2,34}... | collective-permute-start | bytes 36872 | tf_op jit(solution)/shard_map/ppermute | solution.py:540
  189.6 4.9 %collective-permute-start.19 = (bf16[2,8,8,48]{3,2,1,0:T(8,128)(2,1)S(1)}, bf16[2,8,8,48]{3,2,1,0:T(8,128)(2,1)S(1)}, u32[]{:S(2)}, u32[]{:S(2)}) collective-permute-start(bf16[2,8,8,48]{3,2,1,0:T(8,128)(2,1)S(1)} %bitcast.38), channel_id=1, source_target_pairs={{0,96},{32,0},{64,32},{96,64},{1,97},{33,1},{65,33},{97,65},{2,98}... | collective-permute-start | bytes 36872 | tf_op jit(solution)/shard_map/ppermute | solution.py:540
  194.6 5.1 %collective-permute-start.21 = (bf16[4,2,8,48]{3,2,1,0:T(8,128)(2,1)S(1)}, bf16[4,2,8,48]{3,2,1,0:T(8,128)(2,1)S(1)}, u32[]{:S(2)}, u32[]{:S(2)}) collective-permute-start(bf16[4,2,8,48]{3,2,1,0:T(8,128)(2,1)S(1)} %get-tuple-element.48), channel_id=1, source_target_pairs={{0,24},{8,0},{16,8},{24,16},{1,25},{9,1},{17,9},{25,17},{2,26},{10... | collective-permute-start | bytes 18440 | tf_op jit(solution)/shard_map/ppermute | solution.py:540
  194.6 5.1 %collective-permute-start.20 = (bf16[4,2,8,48]{3,2,1,0:T(8,128)(2,1)S(1)}, bf16[4,2,8,48]{3,2,1,0:T(8,128)(2,1)S(1)}, u32[]{:S(2)}, u32[]{:S(2)}) collective-permute-start(bf16[4,2,8,48]{3,2,1,0:T(8,128)(2,1)S(1)} %get-tuple-element.49), channel_id=1, source_target_pairs={{0,8},{8,16},{16,24},{24,0},{1,9},{9,17},{17,25},{25,1},{2,10},{10... | collective-permute-start | bytes 18440 | tf_op jit(solution)/shard_map/ppermute | solution.py:540
  199.8 5.8 %collective-permute-start.22 = (bf16[4,4,2,48]{3,2,1,0:T(2,128)(2,1)S(1)}, bf16[4,4,2,48]{3,2,1,0:T(2,128)(2,1)S(1)}, u32[]{:S(2)}, u32[]{:S(2)}) collective-permute-start(bf16[4,4,2,48]{3,2,1,0:T(2,128)(2,1)S(1)} %get-tuple-element.52), channel_id=1, source_target_pairs={{0,1},{1,2},{2,3},{3,4},{4,5},{5,6},{6,7},{7,0},{8,9},{9,10},{10,1... | collective-permute-start | bytes 9224 | tf_op jit(solution)/shard_map/ppermute | solution.py:540
  200.0 5.6 %collective-permute-start.23 = (bf16[4,4,2,48]{3,2,1,0:T(2,128)(2,1)S(1)}, bf16[4,4,2,48]{3,2,1,0:T(2,128)(2,1)S(1)}, u32[]{:S(2)}, u32[]{:S(2)}) collective-permute-start(bf16[4,4,2,48]{3,2,1,0:T(2,128)(2,1)S(1)} %get-tuple-element.53), channel_id=1, source_target_pairs={{0,7},{1,0},{2,1},{3,2},{4,3},{5,4},{6,5},{7,6},{8,15},{9,8},{10,9... | collective-permute-start | bytes 9224 | tf_op jit(solution)/shard_map/ppermute | solution.py:540

commit v2 on v1

v2 whole, which is shorter than its diff:
```python
import math

import jax
import jax.numpy as jnp
from jax import lax
from jax.experimental import pallas as pl
from jax.experimental.pallas import tpu as pltpu
from jax.sharding import PartitionSpec as P

CX = 4
CY = 4
CZ = 2
PER_CELL = 16
SLOTS = 32
CH = 128
NBASIS = 8
SPECIES = 4

CELL_SIDE = 2.0
CUTOFF = 10.5
NORM_EPS = 1e-05

COLS = CX * CY
PAIRS = CZ * PER_CELL * SLOTS
CELL_PAIRS = PER_CELL * SLOTS
ATOMS = COLS * CZ * PER_CELL
RUN = 48
SLAB = 5 * RUN
CELL_ROWS = 40
OWN_RUNS = CY * (CX + 4)
RIM_RUNS = 2 * (CX + 4)
LANES = PAIRS // 128

F32 = jnp.float32
BF16 = jnp.bfloat16
DEGREE = (0, 1, 1, 1, 2, 2, 2, 2, 2)

F_Y = 0
F_W = 9
F_DW = 10
F_B = 11
F_DB = 19
F_INV = 27
F_COUNT = 28

G_B = 0
G_Y = 8
G_E = 17
G_COUNT = 24


def dims(a, b, ca, cb):
    return lax.dot_general(a, b, (((ca,), (cb,)), ((), ())), preferred_element_type=F32)


def halves(value):
    high = value.astype(BF16)
    return high, (value - high.astype(F32)).astype(BF16)


def dims_three(a, b, ca, cb):
    a_high, a_low = halves(a)
    b_high, b_low = halves(b)
    return dims(a_high, b_high, ca, cb) + (
        dims(a_high, b_low, ca, cb) + dims(a_low, b_high, ca, cb)
    )


def iota(shape, dim):
    return lax.broadcasted_iota(jnp.int32, shape, dim)


def one_hot(condition):
    return jnp.where(condition, 1.0, 0.0).astype(BF16)


def radial_blocks(radial):
    rows = []
    for m in range(9):
        before = [jnp.zeros((NBASIS, m * CH), F32)] if m else []
        after = [jnp.zeros((NBASIS, (8 - m) * CH), F32)] if m < 8 else []
        rows.append(jnp.concatenate(before + [radial] + after, 1))
    return jnp.concatenate(rows, 0)


def looped(count, body, unroll):
    def step(j, carry):
        for k in range(unroll):
            body(j * unroll + k)
        return carry

    lax.fori_loop(0, count // unroll, step, 0)


def sigmoid_of(v):
    return 0.5 * jnp.tanh(0.5 * v) + 0.5


def feature_rows(ref, row, count, i):
    blocks = []
    for lane in range(LANES):
        start = (lane * F_COUNT + row) * COLS + i
        blocks.append(ref[pl.ds(start, count, stride=COLS) if count > 1 else pl.ds(start, 1), :])
    return jnp.concatenate(blocks, 1)


def whole_feature(ref, row):
    blocks = []
    for lane in range(LANES):
        start = (lane * F_COUNT + row) * COLS
        blocks.append(ref[start : start + COLS, :])
    return jnp.concatenate(blocks, 1)


def put_feature(ref, row, value):
    for lane in range(LANES):
        start = (lane * F_COUNT + row) * COLS
        ref[start : start + COLS, :] = value[:, lane * 128 : (lane + 1) * 128]


def cell_window(ref, x, y):
    parts = []
    for dx in range(5):
        start = pl.multiple_of(((x + dx) * 8 + y) * 8, 8)
        parts.append(ref[pl.ds(start, CELL_ROWS), :])
    return jnp.concatenate(parts, 0)


def env_kernel(
    nbr_ref,
    ext_ref,
    own_ref,
    count_ref,
    species_ref,
    embed_ref,
    radial_ref,
    mix_ref,
    hidden_ref,
    env_ref,
    scale_ref,
    feat_ref,
    code_ref,
    near_ref,
    moment_ref,
):
    shape = (COLS, PAIRS)
    number = nbr_ref[...]
    slot = number & 15
    cell = number >> 4
    over = (cell * 43691) >> 18
    cell_z = cell - 6 * over
    cell_y = over & 7
    cell_x = over >> 3
    column = iota(shape, 0)
    lane = iota(shape, 1)
    dx = cell_x - (column >> 2)
    dy = cell_y - (column & 3)
    upper = (cell_z >= 3).astype(jnp.int32)
    code_ref[0] = (dy * 5 + dx) * RUN + (cell_z - 3 * upper) * PER_CELL + slot
    code_ref[1] = upper
    code_ref[2] = dx * CELL_ROWS + dy * 8 + cell_z
    code_ref[3] = slot

    row_cells = iota((5 * CELL_ROWS, PAIRS), 0)
    row_slots = iota((PER_CELL, PAIRS), 0)

    def fetch(i):
        hot = one_hot(row_cells == code_ref[2, pl.ds(i, 1), :])
        high, low = halves(cell_window(ext_ref, i // CY, i % CY))
        places = dims(high, hot, 0, 0) + dims(low, hot, 0, 0)
        mask = row_slots == code_ref[3, pl.ds(i, 1), :]
        for c in range(3):
            part = places[c * PER_CELL : (c + 1) * PER_CELL]
            near_ref[c, pl.ds(i, 1), :] = jnp.sum(jnp.where(mask, part, 0.0), 0, keepdims=True)

    looped(COLS, fetch, 2)

    spread = one_hot(iota((32, PAIRS), 0) == (iota((32, PAIRS), 1) >> 5))
    own_high, own_low = halves(own_ref[...])
    own = dims(own_high, spread, 1, 0) + dims(own_low, spread, 1, 0)
    count = dims(count_ref[...].astype(F32).astype(BF16), spread, 1, 0)
    live = ((lane & 31).astype(F32) < count).astype(F32)
    step_x = (dx - 2).astype(F32) * CELL_SIDE + near_ref[0] - own[0:COLS]
    step_y = (dy - 2).astype(F32) * CELL_SIDE + near_ref[1] - own[COLS : 2 * COLS]
    step_z = (
        (cell_z - 2 - (lane >> 9)).astype(F32) * CELL_SIDE + near_ref[2] - own[2 * COLS : 3 * COLS]
    )
    square = step_x * step_x + step_y * step_y + step_z * step_z
    distance = jnp.sqrt(square)
    inverse = 1.0 / distance
    nx, ny, nz = step_x * inverse, step_y * inverse, step_z * inverse

    def put(row, value):
        put_feature(feat_ref, row, value)

    three, five, fifteen = math.sqrt(3.0), math.sqrt(5.0), math.sqrt(15.0)
    put(F_Y, jnp.ones(shape, F32))
    put(F_Y + 1, three * nx)
    put(F_Y + 2, three * ny)
    put(F_Y + 3, three * nz)
    put(F_Y + 4, fifteen * nx * ny)
    put(F_Y + 5, fifteen * ny * nz)
    put(F_Y + 6, (0.5 * five) * (3.0 * nz * nz - 1.0))
    put(F_Y + 7, fifteen * nx * nz)
    put(F_Y + 8, (0.5 * fifteen) * (nx * nx - ny * ny))
    scaled = distance * (1.0 / CUTOFF)
    inside = 1.0 - scaled * scaled
    put(F_W, live * inside * inside)
    put(F_DW, live * (-4.0 / CUTOFF) * scaled * inside)
    put(F_INV, inverse)
    angle = distance * (math.pi / CUTOFF)
    sine, cosine = jnp.sin(angle), jnp.cos(angle)
    last_s, last_c = jnp.zeros(shape, F32), jnp.ones(shape, F32)
    now_s, now_c = sine, cosine
    for k in range(1, NBASIS + 1):
        basis = CELL_SIDE * now_s * inverse
        put(F_B + k - 1, basis)
        put(F_DB + k - 1, (CELL_SIDE * k * math.pi / CUTOFF * now_c - basis) * inverse)
        last_s, now_s = now_s, 2.0 * cosine * now_s - last_s
        last_c, now_c = now_c, 2.0 * cosine * now_c - last_c

    atoms = one_hot(iota((PER_CELL, CELL_PAIRS), 0) == (iota((PER_CELL, CELL_PAIRS), 1) >> 5))

    def moments(i):
        harmonic = feature_rows(feat_ref, F_Y, 9, i)
        weighted = feature_rows(feat_ref, F_B, NBASIS, i) * feature_rows(feat_ref, F_W, 1, i)
        products = jnp.concatenate([harmonic[m : m + 1] * weighted for m in range(9)], 0)
        high, low = halves(products)
        for z in range(CZ):
            part = slice(z * CELL_PAIRS, (z + 1) * CELL_PAIRS)
            start = pl.multiple_of((i * CZ + z) * PER_CELL, PER_CELL)
            moment_ref[pl.ds(start, PER_CELL), :] = dims(atoms, high[:, part], 1, 1) + dims(
                atoms, low[:, part], 1, 1
            )

    looped(COLS, moments, 2)

    kind = one_hot(iota((SPECIES, ATOMS), 0) == species_ref[...])
    embed_high, embed_low = halves(embed_ref[...] * (1.0 / math.sqrt(SLOTS)))
    scale = dims(kind, embed_high, 0, 0) + dims(kind, embed_low, 0, 0)
    scale_ref[...] = scale
    sums = dims_three(moment_ref[...], radial_blocks(radial_ref[...]), 1, 0)
    invariants = [None] * 3
    for m in range(9):
        value = sums[:, m * CH : (m + 1) * CH] * scale
        env_ref[m] = value
        degree = DEGREE[m]
        squared = value * value
        invariants[degree] = (
            squared if invariants[degree] is None else invariants[degree] + squared
        )
    normed, _ = normalised(invariants)
    mixed = dims(jnp.concatenate(normed, 1).astype(BF16), mix_ref[...], 1, 0)
    hidden = (mixed * sigmoid_of(mixed)).astype(BF16)
    for y in range(CY):
        for x in range(CX):
            hidden_ref[y, x] = hidden[(x * CY + y) * 32 : (x * CY + y + 1) * 32]


def normalised(invariants):
    total = sum(jnp.sum(q * q, 1, keepdims=True) for q in invariants)
    inverse = lax.rsqrt(total * (1.0 / (3 * CH)) + NORM_EPS)
    return [q * inverse for q in invariants], inverse


def spans(z):
    return slice(z * CELL_PAIRS, (z + 1) * CELL_PAIRS)


def rows_of(column, z):
    return pl.ds(pl.multiple_of((column * CZ + z) * PER_CELL, PER_CELL), PER_CELL)


def slab_rows(block, x):
    return pl.ds(pl.multiple_of((block * 8 + x) * RUN, RUN), SLAB)


def fill_table(table_ref, start, around, weights, runs):
    for h in range(2):
        rows = around[:, h].reshape(runs * RUN, CH)
        table_ref[start : start + runs * RUN, h * CH : (h + 1) * CH] = dims(
            rows, weights, 1, 0
        ).astype(BF16)


def atom_blocks():
    mask = iota((PER_CELL, CELL_PAIRS), 0) == (iota((PER_CELL, CELL_PAIRS), 1) >> 5)
    return mask, one_hot(mask)


def pair_features(harmonic, part, mask):
    return [jnp.where(mask, harmonic[m : m + 1, part], 0.0).astype(BF16) for m in range(9)]


def scaled_env(env_ref, couple_ref, column, z):
    rows = rows_of(column, z)
    return [
        (env_ref[m, rows, :] * couple_ref[DEGREE[m] : DEGREE[m] + 1]).astype(BF16)
        for m in range(9)
    ]


def early_kernel(
    around_ref,
    hidden_ref,
    env_ref,
    feat_ref,
    code_ref,
    center_ref,
    neigh_ref,
    radial_ref,
    couple_ref,
    early_ref,
    table_ref,
    own_ref,
):
    y = pl.program_id(0)

    @pl.when(y == 0)
    def _():
        fill_table(table_ref, 0, around_ref, neigh_ref[...], OWN_RUNS)
        for yy in range(CY):
            for x in range(CX):
                start = (x * CY + yy) * 32
                own_ref[start : start + 32, :] = dims(
                    hidden_ref[yy, x], center_ref[...], 1, 0
                )

    radial_high, radial_low = halves(radial_ref[...])
    mask, atoms = atom_blocks()
    row_slab = iota((SLAB, PAIRS), 0)

    def column(x, first, count, block):
        i = x * CY + y
        harmonic = feature_rows(feat_ref, F_Y, 9, i)
        basis_high, basis_low = halves(feature_rows(feat_ref, F_B, NBASIS, i))
        code = code_ref[0, pl.ds(i, 1), :]
        upper = code_ref[1, pl.ds(i, 1), :] > 0
        parts = []
        for z in range(CZ):
            part = spans(z)
            feature = jnp.concatenate(
                pair_features(harmonic, part, mask)
                + [
                    atoms,
                    atoms,
                    basis_high[:, part],
                    basis_low[:, part],
                    basis_high[:, part],
                    jnp.zeros((8, CELL_PAIRS), BF16),
                ],
                0,
            )
            own_high, own_low = halves(own_ref[rows_of(i, z), :])
            table = jnp.concatenate(
                scaled_env(env_ref, couple_ref, i, z)
                + [
                    own_high,
                    own_low,
                    radial_high,
                    radial_high,
                    radial_low,
                    jnp.zeros((8, CH), BF16),
                ],
                0,
            )
            parts.append(dims(table, feature, 0, 0))
        fetched = None
        for k in range(count):
            hot = one_hot(row_slab == code - (first + k) * SLAB)
            found = dims(table_ref[slab_rows(block + k, x), :], hot, 0, 0)
            fetched = found if fetched is None else fetched + found
        early_ref[x] = jnp.concatenate(parts, 1) + jnp.where(upper, fetched[CH:], fetched[:CH])

    @pl.when((y == 0) | (y == 3))
    def _():
        far = (y == 3).astype(jnp.int32)
        looped(CX, lambda x: column(x, 2 - 2 * far, 3, far), 1)

    @pl.when((y == 1) | (y == 2))
    def _():
        looped(CX, lambda x: column(x, 2 - y, 4, 0), 1)


def pair_kernel(
    early_ref,
    low_ref,
    up_ref,
    feat_ref,
    code_ref,
    neigh_ref,
    two_ref,
    three_ref,
    readout_ref,
    energy_ref,
    low_out_ref,
    up_out_ref,
    grad_ref,
    raw_ref,
    table_ref,
    total_ref,
    hot_ref,
):
    y = pl.program_id(0)

    @pl.when(y == 0)
    def _():
        fill_table(table_ref, 0, low_ref, neigh_ref[...], RIM_RUNS)
        fill_table(table_ref, RIM_RUNS * RUN, up_ref, neigh_ref[...], RIM_RUNS)
        total_ref[...] = jnp.zeros_like(total_ref)

    readout = jnp.transpose(jnp.broadcast_to(readout_ref[...], (CH, CH)))
    readout = jnp.concatenate([readout] * LANES, 1)
    row_slab = iota((SLAB, PAIRS), 0)

    def column(x, first, count, block):
        i = x * CY + y
        weight = feature_rows(feat_ref, F_W, 1, i)
        code = code_ref[0, pl.ds(i, 1), :]
        upper = code_ref[1, pl.ds(i, 1), :] > 0
        fetched = None
        for k in range(count):
            hot = one_hot(row_slab == code - (first + k) * SLAB)
            hot_ref[k * SLAB : (k + 1) * SLAB, :] = hot
            found = dims(table_ref[slab_rows(block + k, x), :], hot, 0, 0)
            fetched = found if fetched is None else fetched + found
        value = early_ref[x] + jnp.where(upper, fetched[CH:], fetched[:CH])
        gate = sigmoid_of(value)
        one = value * gate
        slope_one = gate + one - one * gate
        value = dims(two_ref[...], one.astype(BF16), 0, 0)
        gate = sigmoid_of(value)
        two = value * gate
        slope_two = gate + two - two * gate
        value = dims(three_ref[...], two.astype(BF16), 0, 0)
        gate = sigmoid_of(value)
        top = value * gate
        slope_top = gate + top - top * gate
        raw_ref[pl.ds(i, 1), :] = jnp.sum(top * readout, 0, keepdims=True)
        grad = slope_top * readout * weight
        grad = dims(three_ref[...], grad.astype(BF16), 1, 0) * slope_two
        grad = dims(two_ref[...], grad.astype(BF16), 1, 0) * slope_one
        spread = jnp.concatenate(
            [jnp.where(upper, 0.0, grad), jnp.where(upper, grad, 0.0)], 0
        ).astype(BF16)
        grad_ref[x] = grad.astype(BF16)
        found = dims(hot_ref[: count * SLAB, :], spread, 1, 1)
        for k in range(count):
            total_ref[slab_rows(block + k, x), :] += found[k * SLAB : (k + 1) * SLAB]

    @pl.when((y == 0) | (y == 3))
    def _():
        far = (y == 3).astype(jnp.int32)
        looped(CX, lambda x: column(x, 3 * far, 2, 2 * far), 1)

    @pl.when((y == 1) | (y == 2))
    def _():
        looped(CX, lambda x: column(x, 4 * (y - 1), 1, y), 1)

    @pl.when(y == CY - 1)
    def _():
        for h in range(2):
            rim = total_ref[:, h * CH : (h + 1) * CH].astype(BF16).reshape(2 * RIM_RUNS, RUN, CH)
            low_out_ref[:, h] = rim[:RIM_RUNS]
            up_out_ref[:, h] = rim[RIM_RUNS:]
        gather = one_hot(iota((32, PAIRS), 0) == (iota((32, PAIRS), 1) >> 5))
        high, low = halves(raw_ref[...] * whole_feature(feat_ref, F_W))
        energy_ref[...] = dims(high, gather, 1, 1) + dims(low, gather, 1, 1)


def spread_kernel(grad_ref, code_ref, ghost_ref, total_ref, hot_ref):
    y = pl.program_id(0)

    @pl.when(y == 0)
    def _():
        total_ref[...] = jnp.zeros_like(total_ref)

    row_slab = iota((SLAB, PAIRS), 0)

    def column(x, first, count, block):
        i = x * CY + y
        code = code_ref[0, pl.ds(i, 1), :]
        upper = jnp.where(code_ref[1, pl.ds(i, 1), :] > 0, 1.0, 0.0).astype(BF16)
        for k in range(count):
            hot_ref[k * SLAB : (k + 1) * SLAB, :] = one_hot(
                row_slab == code - (first + k) * SLAB
            )
        grad = grad_ref[x]
        high = grad * upper
        spread = jnp.concatenate([grad - high, high], 0)
        found = dims(hot_ref[: count * SLAB, :], spread, 1, 1)
        for k in range(count):
            total_ref[slab_rows(block + k, x), :] += found[k * SLAB : (k + 1) * SLAB]

    @pl.when((y == 0) | (y == 3))
    def _():
        far = (y == 3).astype(jnp.int32)
        looped(CX, lambda x: column(x, 2 - 2 * far, 3, far), 1)

    @pl.when((y == 1) | (y == 2))
    def _():
        looped(CX, lambda x: column(x, 2 - y, 4, 0), 1)

    @pl.when(y == CY - 1)
    def _():
        for h in range(2):
            ghost_ref[:, h] = (
                total_ref[:, h * CH : (h + 1) * CH].astype(BF16).reshape(OWN_RUNS, RUN, CH)
            )


def back_kernel(
    grad_ref,
    env_ref,
    scale_ref,
    feat_ref,
    mix_ref,
    center_ref,
    radial_a_ref,
    radial_ref,
    couple_ref,
    down_ref,
    base_ref,
    slope_ref,
    normed_ref,
    pull_ref,
    direct_ref,
    grad_env_ref,
    grad_center_ref,
):
    y = pl.program_id(0)
    mask, atoms = atom_blocks()
    radial = radial_ref[...].astype(BF16)

    def column(x):
        i = x * CY + y
        harmonic = feature_rows(feat_ref, F_Y, 9, i)
        for z in range(CZ):
            part = spans(z)
            grad = grad_ref[x, :, part]
            feature = jnp.concatenate(pair_features(harmonic, part, mask) + [atoms], 0)
            back = dims(feature, grad, 1, 1)
            for m in range(9):
                grad_env_ref[m, rows_of(i, z), :] = back[m * PER_CELL : (m + 1) * PER_CELL]
            grad_center_ref[rows_of(i, z), :] = back[9 * PER_CELL :]
            table = jnp.concatenate(
                scaled_env(env_ref, couple_ref, i, z) + [radial, jnp.zeros((8, CH), BF16)], 0
            )
            down = dims(table, grad, 1, 0)
            rows = [down[9 * PER_CELL : 9 * PER_CELL + NBASIS]]
            for m in range(9):
                kept = jnp.where(mask, down[m * PER_CELL : (m + 1) * PER_CELL], 0.0)
                rows.append(jnp.sum(kept, 0, keepdims=True))
            down_ref[i, 0 : NBASIS + 9, part] = jnp.concatenate(rows, 0)

    looped(CX, column, 1)

    @pl.when(y == CY - 1)
    def _():
        invariants = [None] * 3
        for m in range(9):
            value = env_ref[m]
            squared = value * value
            degree = DEGREE[m]
            invariants[degree] = (
                squared if invariants[degree] is None else invariants[degree] + squared
            )
        normed, inverse = normalised(invariants)
        mixed = dims(jnp.concatenate(normed, 1).astype(BF16), mix_ref[...], 1, 0)
        gate = sigmoid_of(mixed)
        act = mixed * gate
        slope_ref[...] = gate + act - act * gate
        for d in range(3):
            normed_ref[d] = normed[d]
        high, low = halves(grad_center_ref[...])
        base_ref[...] = dims(high, center_ref[...], 1, 1) + dims(low, center_ref[...], 1, 1)
        scale = scale_ref[...]
        for m in range(9):
            pull_ref[m] = 2.0 * env_ref[m] * scale * inverse
        pulled = [
            grad_env_ref[m] * couple_ref[DEGREE[m] : DEGREE[m] + 1] * scale for m in range(9)
        ]
        direct_ref[...] = dims_three(
            jnp.concatenate(pulled, 1), radial_blocks(radial_a_ref[...]), 1, 1
        )


def force_kernel(
    neigh_ref,
    base_ref,
    slope_ref,
    normed_ref,
    pull_env_ref,
    direct_ref,
    feat_ref,
    code_ref,
    down_ref,
    raw_ref,
    mix_ref,
    proj_ref,
    radial_ref,
    own_ref,
    ghost_ref,
    moment_ref,
    pull_ref,
):
    neigh = jnp.concatenate([neigh_ref[y, x] for x in range(CX) for y in range(CY)], 0)
    high, low = halves(neigh)
    grad = base_ref[...] + dims(high, proj_ref[...], 1, 1) + dims(low, proj_ref[...], 1, 1)
    grad = grad * slope_ref[...]
    grad = dims(grad.astype(BF16), mix_ref[...], 1, 1)
    grads = [grad[:, d * CH : (d + 1) * CH] for d in range(3)]
    normed = [normed_ref[d] for d in range(3)]
    mean = sum(jnp.sum(g * q, 1, keepdims=True) for g, q in zip(grads, normed)) * (1.0 / (3 * CH))
    grads = [g - q * mean for g, q in zip(grads, normed)]
    pulled = [pull_env_ref[m] * grads[DEGREE[m]] for m in range(9)]
    moment_ref[...] = direct_ref[...] + dims_three(
        jnp.concatenate(pulled, 1), radial_blocks(radial_ref[...]), 1, 1
    )

    _, atoms = atom_blocks()
    row_cells = iota((5 * CELL_ROWS, PAIRS), 0)
    row_slots = iota((PER_CELL, PAIRS), 0)
    ghost_ref[...] = jnp.zeros_like(ghost_ref)
    three, five, fifteen = math.sqrt(3.0), math.sqrt(5.0), math.sqrt(15.0)

    def column(i):
        harmonic = feature_rows(feat_ref, F_Y, 9, i)
        basis = feature_rows(feat_ref, F_B, NBASIS, i)
        slope = feature_rows(feat_ref, F_DB, NBASIS, i)
        weight = feature_rows(feat_ref, F_W, 1, i)
        weight_slope = feature_rows(feat_ref, F_DW, 1, i)
        inverse = feature_rows(feat_ref, F_INV, 1, i)
        parts = []
        for z in range(CZ):
            high, low = halves(moment_ref[rows_of(i, z), :])
            parts.append(dims(high, atoms, 0, 0) + dims(low, atoms, 0, 0))
        back = jnp.concatenate(parts, 1)
        weighted = basis * weight
        grad_weighted = jnp.zeros((NBASIS, PAIRS), F32)
        chain = []
        for m in range(9):
            block = back[m * NBASIS : (m + 1) * NBASIS]
            grad_weighted += block * harmonic[m : m + 1]
            if m:
                chain.append(
                    down_ref[i, NBASIS + m : NBASIS + m + 1, :]
                    + jnp.sum(block * weighted, 0, keepdims=True)
                )
        y1, y2, y3, y4, y5, y6, y7, y8 = chain
        grad_basis = down_ref[i, 0:NBASIS, :] + grad_weighted * weight
        grad_weight = raw_ref[pl.ds(i, 1), :] + jnp.sum(grad_weighted * basis, 0, keepdims=True)
        radial = jnp.sum(grad_basis * slope, 0, keepdims=True) + grad_weight * weight_slope
        nx, ny, nz = (harmonic[c : c + 1] * (1.0 / three) for c in range(1, 4))
        grad_x = three * y1 + fifteen * (ny * y4 + nz * y7 + nx * y8)
        grad_y = three * y2 + fifteen * (nx * y4 + nz * y5 - ny * y8)
        grad_z = three * y3 + fifteen * (ny * y5 + nx * y7) + (3.0 * five) * nz * y6
        along = radial - inverse * (nx * grad_x + ny * grad_y + nz * grad_z)
        pulls = (
            grad_x * inverse + nx * along,
            grad_y * inverse + ny * along,
            grad_z * inverse + nz * along,
        )
        x, y = i // CY, i % CY
        hot = one_hot(row_cells == code_ref[2, pl.ds(i, 1), :])
        mask = row_slots == code_ref[3, pl.ds(i, 1), :]
        for c in range(3):
            pull_ref[c, pl.ds(i, 1), :] = pulls[c]
        kept = jnp.concatenate([jnp.where(mask, pull, 0.0) for pull in pulls], 0)
        found = dims(hot, kept.astype(BF16), 1, 1)
        for dx in range(5):
            start = pl.multiple_of(((x + dx) * 8 + y) * 8, 8)
            ghost_ref[pl.ds(start, CELL_ROWS), :] += found[dx * CELL_ROWS : (dx + 1) * CELL_ROWS]

    looped(COLS, column, 2)

    gather = one_hot(iota((32, PAIRS), 0) == (iota((32, PAIRS), 1) >> 5))
    for c in range(3):
        high, low = halves(pull_ref[c])
        own_ref[c] = dims(high, gather, 1, 1) + dims(low, gather, 1, 1)


def call(kernel, outs, scratch, *args, by_y=(), by_y_out=(), micros=20):
    def spec(shape, moving):
        zeros = (0,) * len(shape)
        if not moving:
            return pl.BlockSpec(shape, lambda y: zeros)
        return pl.BlockSpec((shape[0] // CY,) + shape[1:], lambda y: (y,) + zeros[1:])

    grid = {}
    if by_y or by_y_out:
        grid = dict(
            grid=(CY,),
            in_specs=[spec(a.shape, k in by_y) for k, a in enumerate(args)],
            out_specs=[spec(shape, k in by_y_out) for k, (shape, _) in enumerate(outs)],
        )
    return pl.pallas_call(
        kernel,
        out_shape=[jax.ShapeDtypeStruct(shape, dtype) for shape, dtype in outs],
        scratch_shapes=[pltpu.VMEM(shape, dtype) for shape, dtype in scratch],
        compiler_params=pltpu.CompilerParams(vmem_limit_bytes=56 * 2**20),
        cost_estimate=pl.CostEstimate(
            flops=micros * 10**9, bytes_accessed=micros * 3 * 10**6, transcendentals=0
        ),
        **grid,
    )(*args)


def shifted(block, axis, distance):
    size = lax.axis_size(axis)
    return lax.ppermute(block, axis, [(i, (i + distance) % size) for i in range(size)])


def rims(array, axis, dim):
    length = array.shape[dim]
    before = shifted(lax.slice_in_dim(array, length - 2, length, axis=dim), axis, 1)
    after = shifted(lax.slice_in_dim(array, 0, 2, axis=dim), axis, -1)
    return before, after


def padded(array, axis, dim, tail=0):
    before, after = rims(array, axis, dim)
    parts = [before, array, after]
    if tail:
        parts.append(jnp.zeros(after.shape[:dim] + (tail,) + after.shape[dim + 1 :], array.dtype))
    return jnp.concatenate(parts, axis=dim)


def folded(array, axis, dim, length):
    lower = lax.slice_in_dim(array, 0, 2, axis=dim).astype(BF16)
    upper = lax.slice_in_dim(array, length + 2, length + 4, axis=dim).astype(BF16)
    core = lax.slice_in_dim(array, 2, length + 2, axis=dim).astype(F32)
    to_first = shifted(upper, axis, 1).astype(F32)
    to_last = shifted(lower, axis, -1).astype(F32)
    if length == 2:
        return core + to_first + to_last
    return core + jnp.concatenate([to_first, to_last], axis=dim)


def shards(
    offsets,
    species,
    neighbours,
    counts,
    embed,
    radial_a,
    mix_in,
    proj_center,
    proj_neigh,
    radial_b,
    couple,
    latent_two,
    latent_three,
    readout,
):
    numbers = neighbours.reshape(COLS, PAIRS)
    places = offsets.reshape(CX, CY, CZ, 48)
    around = padded(padded(padded(places, "gx", 0), "gy", 1), "gz", 2, tail=2)
    own = offsets.reshape(COLS, CZ, 3, PER_CELL).transpose(2, 0, 1, 3).reshape(3 * COLS, 32)
    hidden, env, scale, feats, codes = call(
        env_kernel,
        [
            ((CY, CX, 32, CH), BF16),
            ((9, ATOMS, CH), F32),
            ((ATOMS, CH), F32),
            ((LANES * F_COUNT * COLS, 128), F32),
            ((4, COLS, PAIRS), jnp.int32),
        ],
        [((3, COLS, PAIRS), F32), ((ATOMS, 72), F32)],
        numbers,
        around.reshape(512, 48),
        own,
        counts.reshape(COLS, 32),
        species.reshape(1, ATOMS),
        embed,
        radial_a,
        mix_in,
    )
    grid = hidden.reshape(CY, CX, CZ, PER_CELL, CH)
    wide = padded(padded(grid, "gz", 2), "gx", 1)
    low, up = rims(wide, "gy", 0)
    (early,) = call(
        early_kernel,
        [((COLS, CH, PAIRS), F32)],
        [((OWN_RUNS * RUN, 2 * CH), BF16), ((ATOMS, CH), F32)],
        wide.reshape(OWN_RUNS, 2, RUN, CH),
        hidden,
        env,
        feats,
        codes,
        proj_center,
        proj_neigh,
        radial_b,
        couple,
        by_y_out=(0,),
    )
    energy, low_back, up_back, grads, raw = call(
        pair_kernel,
        [
            ((COLS, 32), F32),
            ((RIM_RUNS, 2, RUN, CH), BF16),
            ((RIM_RUNS, 2, RUN, CH), BF16),
            ((COLS, CH, PAIRS), BF16),
            ((COLS, PAIRS), F32),
        ],
        [
            ((2 * RIM_RUNS * RUN, 2 * CH), BF16),
            ((2 * RIM_RUNS * RUN, 2 * CH), F32),
            ((2 * SLAB, PAIRS), BF16),
        ],
        early,
        low.reshape(RIM_RUNS, 2, RUN, CH),
        up.reshape(RIM_RUNS, 2, RUN, CH),
        feats,
        codes,
        proj_neigh,
        latent_two,
        latent_three,
        readout.reshape(1, CH),
        by_y=(0,),
        by_y_out=(3,),
    )
    to_first = shifted(up_back, "gy", 1)
    to_last = shifted(low_back, "gy", -1)
    (ghost,) = call(
        spread_kernel,
        [((OWN_RUNS, 2, RUN, CH), BF16)],
        [((OWN_RUNS * RUN, 2 * CH), F32), ((4 * SLAB, PAIRS), BF16)],
        grads,
        codes,
        by_y=(0,),
    )
    ghost = ghost.astype(F32) + jnp.concatenate([to_first, to_last], 0).astype(F32)
    ghost = ghost.reshape(CY, CX + 4, CZ + 4, PER_CELL, CH)
    owned = folded(folded(ghost, "gx", 1, CX), "gz", 2, CZ)
    down, base, slope, normed, pull, direct = call(
        back_kernel,
        [
            ((COLS, 24, PAIRS), F32),
            ((ATOMS, CH), F32),
            ((ATOMS, CH), F32),
            ((3, ATOMS, CH), F32),
            ((9, ATOMS, CH), F32),
            ((ATOMS, 72), F32),
        ],
        [((9, ATOMS, CH), F32), ((ATOMS, CH), F32)],
        grads,
        env,
        scale,
        feats,
        mix_in,
        proj_center,
        radial_a,
        radial_b,
        couple,
        by_y=(0,),
    )
    own_pull, far_pull = call(
        force_kernel,
        [((3, COLS, 32), F32), ((512, 48), F32)],
        [((ATOMS, 72), F32), ((3, COLS, PAIRS), F32)],
        owned.reshape(CY, CX, 32, CH),
        base,
        slope,
        normed,
        pull,
        direct,
        feats,
        codes,
        down,
        raw,
        mix_in,
        proj_neigh,
        radial_a,
    )
    far = far_pull.reshape(CX + 4, CY + 4, 8, 48)
    far = folded(folded(folded(far, "gx", 0, CX), "gy", 1, CY), "gz", 2, CZ)
    near = own_pull.reshape(3, CX, CY, CZ, PER_CELL).transpose(1, 2, 3, 0, 4)
    forces = near - far.reshape(CX, CY, CZ, 3, PER_CELL)
    return (forces, energy.reshape(CX, CY, CZ, PER_CELL))


def solution(mesh):
    placed = (
        P("gx", "gy", "gz", None, None),
        P("gx", "gy", "gz", None),
        P("gx", "gy", "gz", None, None),
        P("gx", "gy", "gz", None),
    ) + (P(),) * 10
    return jax.shard_map(
        shards,
        mesh=mesh,
        in_specs=placed,
        out_specs=(P("gx", "gy", "gz", None, None), P("gx", "gy", "gz", None)),
        check_vma=False,
    )
```

time: 210 us -> 191 us (0.910); the launches traced: 206 us -> 190 us
  waiting for transfers between devices: 55.7 us -> 29.1 us
  Pallas kernels: 89.5 us -> 104 us
    ppermute x24, waiting for transfers between devices: 55.7 us -> 29.1 us  [shifted(): lax.ppermute(block, axis, [(i, (i + distance) % size) for i in range(size)])]
    pallas_call x3 -> x6, Pallas kernels: 89.5 us -> 104 us  [call(): pl.pallas_call(kernel, out_shape=[jax.ShapeDtypeStruct(shape, dtype) for...]
    concatenate x5 -> x4, other arithmetic: 4.16 us -> 1.9 us  [padded(): return jnp.concatenate(parts, axis=dim)]
    slice x14 -> x9, local copies, waits for them, and re-layouts: 4.23 us -> 2.06 us  [the longest x4 1.02 us: rims(): after = shifted(lax.slice_in_dim(array, 0, 2, axis=dim), axis, -1)]
  transfers between devices with their start and end apart: 24 -> 24, of which waited for: 18 -> 16; matrix products, arithmetic and copies ran while one was open for 4% -> 5% of each run, Pallas kernels for 0% -> 24%
where the time goes in v2:
time: 191 us; the launch traced here: 190 us
  Pallas kernels  104 us (54%)
  starting transfers between devices  38.8 us (20%)
  waiting for transfers between devices  29.1 us (15%)
  local copies, waits for them, and re-layouts  12.3 us (6%)
  other arithmetic  5.31 us (3%)
    pallas_call x6, Pallas kernels, call(): pl.pallas_call(kernel, out_shape=[jax.ShapeDtypeStruct(shape, dtype) for...  104 us
    ppermute x24, starting transfers between devices, shifted(): lax.ppermute(block, axis, [(i, (i + distance) % size) for i in range(size)])  38.8 us
    ppermute x24, waiting for transfers between devices, shifted(): lax.ppermute(block, axis, [(i, (i + distance) % size) for i in range(size)])  29.1 us
  transfers between devices with their start and end apart: 24, of which 16 were waited for; matrix products, arithmetic and copies ran while one was open for 5% of the time, Pallas kernels for 24%

profile of v2, /device:TPU:6, one launch (start us, length us, event | category | flops | bytes accessed | tf_op | source)
XLA Modules:
  0.0 190.2 jit_solution(3630364728161992930)
XLA Ops:
  0.6 0.8 fusion.11
  1.7 3.4 %collective-permute-start.1 = (f32[2,4,2,48]{3,2,1,0:T(2,128)S(1)}, f32[2,4,2,48]{3,2,1,0:T(2,128)S(1)}, u32[]{:S(2)}, u32[]{:S(2)}) collective-permute-start(f32[2,4,2,48]{3,2,1,0:T(2,128)S(1)} %slice.93), channel_id=1, source_target_pairs={{0,96},{32,0},{64,32},{96,64},{1,97},{33,1},{65,33},{97,65},{2,98}... | collective-permute-start | bytes 9224 | tf_op jit(solution)/shard_map/ppermute | solution.py:711
  5.1 0.8 copy.19
  7.0 1.5 collective-permute-start.3
  8.5 1.7 collective-permute-done.2
  10.3 1.7 collective-permute-done.3
  12.0 4.3 %collective-permute-start.5 = (f32[8,8,2,48]{3,2,1,0:T(2,128)S(1)}, f32[8,8,2,48]{3,2,1,0:T(2,128)S(1)}, u32[]{:S(2)}, u32[]{:S(2)}) collective-permute-start(f32[8,8,2,48]{3,2,1,0:T(2,128)S(1)} %pad_maximum_fusion.2), channel_id=1, source_target_pairs={{0,7},{1,0},{2,1},{3,2},{4,3},{5,4},{6,5},{7,6},{8,15},{9,8},{10,9... | collective-permute-start | bytes 73736 | tf_op jit(solution)/shard_map/ppermute | solution.py:711
  16.3 0.8 copy_bitcast_fusion
  17.2 1.4 reshape.69.species_ref
  18.5 1.4 reshape.68.count_ref
  19.9 0.7 reshape.67.own_ref
  20.6 1.7 reshape.63.nbr_ref
  22.4 0.7 collective-permute-done.4
  23.1 0.8 maximum_maximum_fusion
  23.9 11.7 %shard_map.149 = (bf16[4,4,32,128]{3,2,1,0:T(8,128)(2,1)}, f32[9,512,128]{2,1,0:T(8,128)}, f32[512,128]{1,0:T(8,128)}, f32[3584,128]{1,0:T(8,128)}, s32[4,16,1024]{2,1,0:T(8,128)}) custom-call(s32[16,1024]{1,0:T(8,128)} %reshape.63.nbr_ref, f32[512,48]{1,0:T(8,128)} %bitcast.29, f32[48,32]{1,0:T(8,128)} %reshape.67.own_ref, s32[16,32]{1,0:T(8,128)} %reshape.68.count_ref, ...), custom_call_target="tpu_custom_call" | custom-call | flops 20000000000 | bytes 60000000 | tf_op jit(solution)/shard_map/pallas_call | solution.py:697
  35.7 3.5 %collective-permute-start.7 = (bf16[4,4,2,16,128]{4,3,2,1,0:T(8,128)(2,1)}, bf16[4,4,2,16,128]{4,3,2,1,0:T(8,128)(2,1)S(1)}, u32[]{:S(2)}, u32[]{:S(2)}) collective-permute-start(bf16[4,4,2,16,128]{4,3,2,1,0:T(8,128)(2,1)} %bitcast.24), channel_id=1, source_target_pairs={{0,7},{1,0},{2,1},{3,2},{4,3},{5,4},{6,5},{7,6},{8,15},{9,8},{10,9... | collective-permute-start | bytes 393224 | tf_op jit(solution)/shard_map/ppermute | solution.py:711
  39.2 4.1 %collective-permute-done.7 = bf16[4,4,2,16,128]{4,3,2,1,0:T(8,128)(2,1)S(1)} collective-permute-done((bf16[4,4,2,16,128]{4,3,2,1,0:T(8,128)(2,1)}, bf16[4,4,2,16,128]{4,3,2,1,0:T(8,128)(2,1)S(1)}, u32[]{:S(2)}, u32[]{:S(2)}) %collective-permute-start.7) | collective-permute-done | bytes 131104 | tf_op jit(solution)/shard_map/ppermute | solution.py:711
  43.3 4.4 %collective-permute-done.6 = bf16[4,4,2,16,128]{4,3,2,1,0:T(8,128)(2,1)S(1)} collective-permute-done((bf16[4,4,2,16,128]{4,3,2,1,0:T(8,128)(2,1)}, bf16[4,4,2,16,128]{4,3,2,1,0:T(8,128)(2,1)S(1)}, u32[]{:S(2)}, u32[]{:S(2)}) %collective-permute-start.6) | collective-permute-done | bytes 131104 | tf_op jit(solution)/shard_map/ppermute | solution.py:711
  47.7 0.9 pad_maximum_fusion.1
  48.7 3.2 %collective-permute-start.9 = (bf16[4,2,6,16,128]{4,3,2,1,0:T(8,128)(2,1)S(1)}, bf16[4,2,6,16,128]{4,3,2,1,0:T(8,128)(2,1)S(1)}, u32[]{:S(2)}, u32[]{:S(2)}) collective-permute-start(bf16[4,2,6,16,128]{4,3,2,1,0:T(8,128)(2,1)S(1)} %get-tuple-element.53), channel_id=1, source_target_pairs={{0,96},{32,0},{64,32},{96,64},{1,97},{33,1},{65,33},{97,65},{2,98}... | collective-permute-start | bytes 589832 | tf_op jit(solution)/shard_map/ppermute | solution.py:711
  52.0 3.3 %collective-permute-done.8 = bf16[4,2,6,16,128]{4,3,2,1,0:T(8,128)(2,1)S(1)} collective-permute-done((bf16[4,2,6,16,128]{4,3,2,1,0:T(8,128)(2,1)S(1)}, bf16[4,2,6,16,128]{4,3,2,1,0:T(8,128)(2,1)S(1)}, u32[]{:S(2)}, u32[]{:S(2)}) %collective-permute-start.8) | collective-permute-done | bytes 196640 | tf_op jit(solution)/shard_map/ppermute | solution.py:711
  56.5 2.9 %collective-permute-start.10 = (bf16[2,8,6,16,128]{4,3,2,1,0:T(8,128)(2,1)S(1)}, bf16[2,8,6,16,128]{4,3,2,1,0:T(8,128)(2,1)S(1)}, u32[]{:S(2)}, u32[]{:S(2)}) collective-permute-start(bf16[2,8,6,16,128]{4,3,2,1,0:T(8,128)(2,1)S(1)} %get-tuple-element.49), channel_id=1, source_target_pairs={{0,8},{8,16},{16,24},{24,0},{1,9},{9,17},{17,25},{25,1},{2,10},{10... | collective-permute-start | bytes 1179656 | tf_op jit(solution)/shard_map/ppermute | solution.py:711
  59.4 17.9 %shard_map.150.early_ref = f32[16,128,1024]{2,1,0:T(8,128)} custom-call(bf16[32,2,48,128]{3,2,1,0:T(8,128)(2,1)} %bitcast.22, bf16[4,4,32,128]{3,2,1,0:T(8,128)(2,1)} %get-tuple-element.20.hidden_ref, f32[9,512,128]{2,1,0:T(8,128)} %get-tuple-element.21.env_ref, f32[3584,128]{1,0:T(8,128)} %get-tuple-element.22.feat_ref, ...), custom_call_target="tpu_custom_call" | custom-call | flops 20000000000 | bytes 60000000 | tf_op jit(solution)/shard_map/pallas_call | solution.py:697
  77.3 0.7 copy-done.3
  78.1 31.6 %shard_map.151 = (f32[16,32]{1,0:T(8,128)}, bf16[16,2,48,128]{3,2,1,0:T(8,128)(2,1)}, bf16[16,2,48,128]{3,2,1,0:T(8,128)(2,1)}, bf16[16,128,1024]{2,1,0:T(8,128)(2,1)}, f32[16,1024]{1,0:T(8,128)}) custom-call(f32[16,128,1024]{2,1,0:T(8,128)} %shard_map.150.early_ref, bf16[16,2,48,128]{3,2,1,0:T(8,128)(2,1)} %bitcast.33, bf16[16,2,48,128]{3,2,1,0:T(8,128)(2,1)} %bitcast.32, ...), custom_call_target="tpu_custom_call" | custom-call | flops 20000000000 | bytes 60000000 | tf_op jit(solution)/shard_map/pallas_call | solution.py:697
  109.8 2.0 %collective-permute-start.13 = (bf16[16,2,48,128]{3,2,1,0:T(8,128)(2,1)}, bf16[16,2,48,128]{3,2,1,0:T(8,128)(2,1)S(1)}, u32[]{:S(2)}, u32[]{:S(2)}) collective-permute-start(bf16[16,2,48,128]{3,2,1,0:T(8,128)(2,1)} %get-tuple-element.26), channel_id=1, source_target_pairs={{0,24},{8,0},{16,8},{24,16},{1,25},{9,1},{17,9},{25,17},{2,26},{10... | collective-permute-start | bytes 1179656 | tf_op jit(solution)/shard_map/ppermute | solution.py:711
  111.8 14.9 %shard_map.152 = bf16[32,2,48,128]{3,2,1,0:T(8,128)(2,1)} custom-call(bf16[16,128,1024]{2,1,0:T(8,128)(2,1)} %get-tuple-element.24.grad_ref, s32[4,16,1024]{2,1,0:T(8,128)} %get-tuple-element.23.code_ref), custom_call_target="tpu_custom_call" | custom-call | flops 20000000000 | bytes 60000000 | tf_op jit(solution)/shard_map/pallas_call | solution.py:697
  126.7 1.4 convert_add_fusion
  128.2 0.9 collective-permute-start.14
  129.1 2.4 %collective-permute-start.15 = (bf16[4,2,6,16,128]{4,3,2,1,0:T(8,128)(2,1)S(1)}, bf16[4,2,6,16,128]{4,3,2,1,0:T(8,128)(2,1)S(1)}, u32[]{:S(2)}, u32[]{:S(2)}) collective-permute-start(bf16[4,2,6,16,128]{4,3,2,1,0:T(8,128)(2,1)S(1)} %get-tuple-element.47), channel_id=1, source_target_pairs={{0,96},{32,0},{64,32},{96,64},{1,97},{33,1},{65,33},{97,65},{2,98}... | collective-permute-start | bytes 589832 | tf_op jit(solution)/shard_map/ppermute | solution.py:711
  131.5 3.3 %collective-permute-done.14 = bf16[4,2,6,16,128]{4,3,2,1,0:T(8,128)(2,1)S(1)} collective-permute-done((bf16[4,2,6,16,128]{4,3,2,1,0:T(8,128)(2,1)S(1)}, bf16[4,2,6,16,128]{4,3,2,1,0:T(8,128)(2,1)S(1)}, u32[]{:S(2)}, u32[]{:S(2)}) %collective-permute-start.14) | collective-permute-done | bytes 196640 | tf_op jit(solution)/shard_map/ppermute | solution.py:711
  135.7 4.1 %collective-permute-start.17 = (bf16[4,4,2,16,128]{4,3,2,1,0:T(8,128)(2,1)S(1)}, bf16[4,4,2,16,128]{4,3,2,1,0:T(8,128)(2,1)S(1)}, u32[]{:S(2)}, u32[]{:S(2)}) collective-permute-start(bf16[4,4,2,16,128]{4,3,2,1,0:T(8,128)(2,1)S(1)} %get-tuple-element.51), channel_id=1, source_target_pairs={{0,7},{1,0},{2,1},{3,2},{4,3},{5,4},{6,5},{7,6},{8,15},{9,8},{10,9... | collective-permute-start | bytes 393224 | tf_op jit(solution)/shard_map/ppermute | solution.py:711
  139.8 12.4 %shard_map.153 = (f32[16,24,1024]{2,1,0:T(8,128)}, f32[512,128]{1,0:T(8,128)}, f32[512,128]{1,0:T(8,128)}, f32[3,512,128]{2,1,0:T(8,128)}, f32[9,512,128]{2,1,0:T(8,128)}, /*index=5*/f32[512,72]{1,0:T(8,128)}) custom-call(bf16[16,128,1024]{2,1,0:T(8,128)(2,1)} %get-tuple-element.24.grad_ref, f32[9,512,128]{2,1,0:T(8,128)} %get-tuple-element.21.env_ref, ...), custom_call_target="tpu_custom_call" | custom-call | flops 20000000000 | bytes 60000000 | tf_op jit(solution)/shard_map/pallas_call | solution.py:697
  152.2 0.7 fusion
  153.0 15.5 %shard_map.154 = (f32[3,16,32]{2,1,0:T(8,128)}, f32[512,48]{1,0:T(8,128)}) custom-call(f32[4,4,32,128]{3,2,1,0:T(8,128)} %bitcast.28, f32[512,128]{1,0:T(8,128)} %get-tuple-element.28.base_ref, f32[512,128]{1,0:T(8,128)} %get-tuple-element.29.slope_ref, f32[3,512,128]{2,1,0:T(8,128)} %get-tuple-element.30.normed_ref, ...), custom_call_target="tpu_custom_call" | custom-call | flops 20000000000 | bytes 60000000 | tf_op jit(solution)/shard_map/pallas_call | solution.py:697
  168.4 1.0 convert.25
  169.4 2.9 %collective-permute-start.19 = (bf16[2,8,8,48]{3,2,1,0:T(8,128)(2,1)S(1)}, bf16[2,8,8,48]{3,2,1,0:T(8,128)(2,1)S(1)}, u32[]{:S(2)}, u32[]{:S(2)}) collective-permute-start(bf16[2,8,8,48]{3,2,1,0:T(8,128)(2,1)S(1)} %bitcast.31), channel_id=1, source_target_pairs={{0,96},{32,0},{64,32},{96,64},{1,97},{33,1},{65,33},{97,65},{2,98}... | collective-permute-start | bytes 36872 | tf_op jit(solution)/shard_map/ppermute | solution.py:711
  172.3 0.9 slice.106
  173.3 0.7 collective-permute-done.19
  173.9 3.2 %collective-permute-done.18 = bf16[2,8,8,48]{3,2,1,0:T(8,128)(2,1)S(1)} collective-permute-done((bf16[2,8,8,48]{3,2,1,0:T(8,128)(2,1)S(1)}, bf16[2,8,8,48]{3,2,1,0:T(8,128)(2,1)S(1)}, u32[]{:S(2)}, u32[]{:S(2)}) %collective-permute-start.18) | collective-permute-done | bytes 12320 | tf_op jit(solution)/shard_map/ppermute | solution.py:711
  177.2 1.4 collective-permute-start.20
  178.6 0.7 collective-permute-start.21
  179.3 1.7 collective-permute-done.20
  181.0 2.5 %collective-permute-done.21 = bf16[4,2,8,48]{3,2,1,0:T(8,128)(2,1)S(1)} collective-permute-done((bf16[4,2,8,48]{3,2,1,0:T(8,128)(2,1)S(1)}, bf16[4,2,8,48]{3,2,1,0:T(8,128)(2,1)S(1)}, u32[]{:S(2)}, u32[]{:S(2)}) %collective-permute-start.21) | collective-permute-done | bytes 6176 | tf_op jit(solution)/shard_map/ppermute | solution.py:711
  183.7 4.1 %collective-permute-start.23 = (bf16[4,4,2,48]{3,2,1,0:T(2,128)(2,1)S(1)}, bf16[4,4,2,48]{3,2,1,0:T(2,128)(2,1)S(1)}, u32[]{:S(2)}, u32[]{:S(2)}) collective-permute-start(bf16[4,4,2,48]{3,2,1,0:T(2,128)(2,1)S(1)} %get-tuple-element.61), channel_id=1, source_target_pairs={{0,7},{1,0},{2,1},{3,2},{4,3},{5,4},{6,5},{7,6},{8,15},{9,8},{10,9... | collective-permute-start | bytes 9224 | tf_op jit(solution)/shard_map/ppermute | solution.py:711
  187.8 0.7 reshape.79
  188.5 0.8 reshape.77
  189.6 0.6 copy.23
  (59 shorter events, 4.3 us)
Async XLA Ops:
  1.5 4.7 %collective-permute-start = (f32[2,4,2,48]{3,2,1,0:T(2,128)S(1)}, f32[2,4,2,48]{3,2,1,0:T(2,128)S(1)}, u32[]{:S(2)}, u32[]{:S(2)}) collective-permute-start(f32[2,4,2,48]{3,2,1,0:T(2,128)S(1)} %slice.91), channel_id=1, source_target_pairs={{0,32},{32,64},{64,96},{96,0},{1,33},{33,65},{65,97},{97,1},{2,34}... | collective-permute-start | bytes 9224 | tf_op jit(solution)/shard_map/ppermute | solution.py:711
  1.7 4.7 %collective-permute-start.1 = (f32[2,4,2,48]{3,2,1,0:T(2,128)S(1)}, f32[2,4,2,48]{3,2,1,0:T(2,128)S(1)}, u32[]{:S(2)}, u32[]{:S(2)}) collective-permute-start(f32[2,4,2,48]{3,2,1,0:T(2,128)S(1)} %slice.93), channel_id=1, source_target_pairs={{0,96},{32,0},{64,32},{96,64},{1,97},{33,1},{65,33},{97,65},{2,98}... | collective-permute-start | bytes 9224 | tf_op jit(solution)/shard_map/ppermute | solution.py:711
  6.5 3.8 %collective-permute-start.2 = (f32[8,2,2,48]{3,2,1,0:T(2,128)S(1)}, f32[8,2,2,48]{3,2,1,0:T(2,128)S(1)}, u32[]{:S(2)}, u32[]{:S(2)}) collective-permute-start(f32[8,2,2,48]{3,2,1,0:T(2,128)S(1)} %get-tuple-element.62), channel_id=1, source_target_pairs={{0,8},{8,16},{16,24},{24,0},{1,9},{9,17},{17,25},{25,1},{2,10},{10... | collective-permute-start | bytes 18440 | tf_op jit(solution)/shard_map/ppermute | solution.py:711
  7.0 4.9 %collective-permute-start.3 = (f32[8,2,2,48]{3,2,1,0:T(2,128)S(1)}, f32[8,2,2,48]{3,2,1,0:T(2,128)S(1)}, u32[]{:S(2)}, u32[]{:S(2)}) collective-permute-start(f32[8,2,2,48]{3,2,1,0:T(2,128)S(1)} %get-tuple-element.63), channel_id=1, source_target_pairs={{0,24},{8,0},{16,8},{24,16},{1,25},{9,1},{17,9},{25,17},{2,26},{10... | collective-permute-start | bytes 18440 | tf_op jit(solution)/shard_map/ppermute | solution.py:711
  12.0 10.4 %collective-permute-start.5 = (f32[8,8,2,48]{3,2,1,0:T(2,128)S(1)}, f32[8,8,2,48]{3,2,1,0:T(2,128)S(1)}, u32[]{:S(2)}, u32[]{:S(2)}) collective-permute-start(f32[8,8,2,48]{3,2,1,0:T(2,128)S(1)} %pad_maximum_fusion.2), channel_id=1, source_target_pairs={{0,7},{1,0},{2,1},{3,2},{4,3},{5,4},{6,5},{7,6},{8,15},{9,8},{10,9... | collective-permute-start | bytes 73736 | tf_op jit(solution)/shard_map/ppermute | solution.py:711
  16.3 6.8 %collective-permute-start.4 = (f32[8,8,2,48]{3,2,1,0:T(2,128)S(1)}, f32[8,8,2,48]{3,2,1,0:T(2,128)S(1)}, u32[]{:S(2)}, u32[]{:S(2)}) collective-permute-start(f32[8,8,2,48]{3,2,1,0:T(2,128)S(1)} %pad_maximum_fusion.2), channel_id=1, source_target_pairs={{0,1},{1,2},{2,3},{3,4},{4,5},{5,6},{6,7},{7,0},{8,9},{9,10},{10,1... | collective-permute-start | bytes 73736 | tf_op jit(solution)/shard_map/ppermute | solution.py:711
  35.6 20.2 %copy-start.1 = (bf16[4,4,32,128]{3,2,1,0:T(8,128)(2,1)S(1)}, bf16[4,4,32,128]{3,2,1,0:T(8,128)(2,1)}, u32[]{:S(2)}) copy-start(bf16[4,4,32,128]{3,2,1,0:T(8,128)(2,1)} %get-tuple-element.20.hidden_ref) | copy-start | bytes 393220
  35.7 7.7 %collective-permute-start.7 = (bf16[4,4,2,16,128]{4,3,2,1,0:T(8,128)(2,1)}, bf16[4,4,2,16,128]{4,3,2,1,0:T(8,128)(2,1)S(1)}, u32[]{:S(2)}, u32[]{:S(2)}) collective-permute-start(bf16[4,4,2,16,128]{4,3,2,1,0:T(8,128)(2,1)} %bitcast.24), channel_id=1, source_target_pairs={{0,7},{1,0},{2,1},{3,2},{4,3},{5,4},{6,5},{7,6},{8,15},{9,8},{10,9... | collective-permute-start | bytes 393224 | tf_op jit(solution)/shard_map/ppermute | solution.py:711
  39.2 8.5 %collective-permute-start.6 = (bf16[4,4,2,16,128]{4,3,2,1,0:T(8,128)(2,1)}, bf16[4,4,2,16,128]{4,3,2,1,0:T(8,128)(2,1)S(1)}, u32[]{:S(2)}, u32[]{:S(2)}) collective-permute-start(bf16[4,4,2,16,128]{4,3,2,1,0:T(8,128)(2,1)} %bitcast.25), channel_id=1, source_target_pairs={{0,1},{1,2},{2,3},{3,4},{4,5},{5,6},{6,7},{7,0},{8,9},{9,10},{10,1... | collective-permute-start | bytes 393224 | tf_op jit(solution)/shard_map/ppermute | solution.py:711
  48.7 6.7 %collective-permute-start.8 = (bf16[4,2,6,16,128]{4,3,2,1,0:T(8,128)(2,1)S(1)}, bf16[4,2,6,16,128]{4,3,2,1,0:T(8,128)(2,1)S(1)}, u32[]{:S(2)}, u32[]{:S(2)}) collective-permute-start(bf16[4,2,6,16,128]{4,3,2,1,0:T(8,128)(2,1)S(1)} %get-tuple-element.52), channel_id=1, source_target_pairs={{0,32},{32,64},{64,96},{96,0},{1,33},{33,65},{65,97},{97,1},{2,34}... | collective-permute-start | bytes 589832 | tf_op jit(solution)/shard_map/ppermute | solution.py:711
  48.7 7.1 %collective-permute-start.9 = (bf16[4,2,6,16,128]{4,3,2,1,0:T(8,128)(2,1)S(1)}, bf16[4,2,6,16,128]{4,3,2,1,0:T(8,128)(2,1)S(1)}, u32[]{:S(2)}, u32[]{:S(2)}) collective-permute-start(bf16[4,2,6,16,128]{4,3,2,1,0:T(8,128)(2,1)S(1)} %get-tuple-element.53), channel_id=1, source_target_pairs={{0,96},{32,0},{64,32},{96,64},{1,97},{33,1},{65,33},{97,65},{2,98}... | collective-permute-start | bytes 589832 | tf_op jit(solution)/shard_map/ppermute | solution.py:711
  55.9 3.5 %copy-start = (bf16[4,8,6,16,128]{4,3,2,1,0:T(8,128)(2,1)}, bf16[4,8,6,16,128]{4,3,2,1,0:T(8,128)(2,1)S(1)}, u32[]{:S(2)}) copy-start(bf16[4,8,6,16,128]{4,3,2,1,0:T(8,128)(2,1)S(1)} %pad_maximum_fusion) | copy-start | bytes 2359300
  56.1 21.2 %collective-permute-start.11 = (bf16[2,8,6,16,128]{4,3,2,1,0:T(8,128)(2,1)S(1)}, bf16[2,8,6,16,128]{4,3,2,1,0:T(8,128)(2,1)S(1)}, u32[]{:S(2)}, u32[]{:S(2)}) collective-permute-start(bf16[2,8,6,16,128]{4,3,2,1,0:T(8,128)(2,1)S(1)} %get-tuple-element.48), channel_id=1, source_target_pairs={{0,24},{8,0},{16,8},{24,16},{1,25},{9,1},{17,9},{25,17},{2,26},{10... | collective-permute-start | bytes 1179656 | tf_op jit(solution)/shard_map/ppermute | solution.py:711
  56.5 20.8 %collective-permute-start.10 = (bf16[2,8,6,16,128]{4,3,2,1,0:T(8,128)(2,1)S(1)}, bf16[2,8,6,16,128]{4,3,2,1,0:T(8,128)(2,1)S(1)}, u32[]{:S(2)}, u32[]{:S(2)}) collective-permute-start(bf16[2,8,6,16,128]{4,3,2,1,0:T(8,128)(2,1)S(1)} %get-tuple-element.49), channel_id=1, source_target_pairs={{0,8},{8,16},{16,24},{24,0},{1,9},{9,17},{17,25},{25,1},{2,10},{10... | collective-permute-start | bytes 1179656 | tf_op jit(solution)/shard_map/ppermute | solution.py:711
  77.3 0.8 copy-start.3
  77.3 0.9 copy-start.4
  109.7 16.9 %collective-permute-start.12 = (bf16[16,2,48,128]{3,2,1,0:T(8,128)(2,1)}, bf16[16,2,48,128]{3,2,1,0:T(8,128)(2,1)S(1)}, u32[]{:S(2)}, u32[]{:S(2)}) collective-permute-start(bf16[16,2,48,128]{3,2,1,0:T(8,128)(2,1)} %get-tuple-element.25), channel_id=1, source_target_pairs={{0,8},{8,16},{16,24},{24,0},{1,9},{9,17},{17,25},{25,1},{2,10},{10... | collective-permute-start | bytes 1179656 | tf_op jit(solution)/shard_map/ppermute | solution.py:711
  109.8 16.9 %collective-permute-start.13 = (bf16[16,2,48,128]{3,2,1,0:T(8,128)(2,1)}, bf16[16,2,48,128]{3,2,1,0:T(8,128)(2,1)S(1)}, u32[]{:S(2)}, u32[]{:S(2)}) collective-permute-start(bf16[16,2,48,128]{3,2,1,0:T(8,128)(2,1)} %get-tuple-element.26), channel_id=1, source_target_pairs={{0,24},{8,0},{16,8},{24,16},{1,25},{9,1},{17,9},{25,17},{2,26},{10... | collective-permute-start | bytes 1179656 | tf_op jit(solution)/shard_map/ppermute | solution.py:711
  128.2 6.7 %collective-permute-start.14 = (bf16[4,2,6,16,128]{4,3,2,1,0:T(8,128)(2,1)S(1)}, bf16[4,2,6,16,128]{4,3,2,1,0:T(8,128)(2,1)S(1)}, u32[]{:S(2)}, u32[]{:S(2)}) collective-permute-start(bf16[4,2,6,16,128]{4,3,2,1,0:T(8,128)(2,1)S(1)} %get-tuple-element.46), channel_id=1, source_target_pairs={{0,32},{32,64},{64,96},{96,0},{1,33},{33,65},{65,97},{97,1},{2,34}... | collective-permute-start | bytes 589832 | tf_op jit(solution)/shard_map/ppermute | solution.py:711
  129.1 6.3 %collective-permute-start.15 = (bf16[4,2,6,16,128]{4,3,2,1,0:T(8,128)(2,1)S(1)}, bf16[4,2,6,16,128]{4,3,2,1,0:T(8,128)(2,1)S(1)}, u32[]{:S(2)}, u32[]{:S(2)}) collective-permute-start(bf16[4,2,6,16,128]{4,3,2,1,0:T(8,128)(2,1)S(1)} %get-tuple-element.47), channel_id=1, source_target_pairs={{0,96},{32,0},{64,32},{96,64},{1,97},{33,1},{65,33},{97,65},{2,98}... | collective-permute-start | bytes 589832 | tf_op jit(solution)/shard_map/ppermute | solution.py:711
  135.6 16.6 %collective-permute-start.16 = (bf16[4,4,2,16,128]{4,3,2,1,0:T(8,128)(2,1)S(1)}, bf16[4,4,2,16,128]{4,3,2,1,0:T(8,128)(2,1)S(1)}, u32[]{:S(2)}, u32[]{:S(2)}) collective-permute-start(bf16[4,4,2,16,128]{4,3,2,1,0:T(8,128)(2,1)S(1)} %get-tuple-element.50), channel_id=1, source_target_pairs={{0,1},{1,2},{2,3},{3,4},{4,5},{5,6},{6,7},{7,0},{8,9},{9,10},{10,1... | collective-permute-start | bytes 393224 | tf_op jit(solution)/shard_map/ppermute | solution.py:711
  135.7 16.5 %collective-permute-start.17 = (bf16[4,4,2,16,128]{4,3,2,1,0:T(8,128)(2,1)S(1)}, bf16[4,4,2,16,128]{4,3,2,1,0:T(8,128)(2,1)S(1)}, u32[]{:S(2)}, u32[]{:S(2)}) collective-permute-start(bf16[4,4,2,16,128]{4,3,2,1,0:T(8,128)(2,1)S(1)} %get-tuple-element.51), channel_id=1, source_target_pairs={{0,7},{1,0},{2,1},{3,2},{4,3},{5,4},{6,5},{7,6},{8,15},{9,8},{10,9... | collective-permute-start | bytes 393224 | tf_op jit(solution)/shard_map/ppermute | solution.py:711
  153.0 34.8 %copy-start.2 = (f32[16,32]{1,0:T(8,128)S(1)}, f32[16,32]{1,0:T(8,128)}, u32[]{:S(2)}) copy-start(f32[16,32]{1,0:T(8,128)} %get-tuple-element.37) | copy-start | bytes 6148
  169.4 4.5 %collective-permute-start.19 = (bf16[2,8,8,48]{3,2,1,0:T(8,128)(2,1)S(1)}, bf16[2,8,8,48]{3,2,1,0:T(8,128)(2,1)S(1)}, u32[]{:S(2)}, u32[]{:S(2)}) collective-permute-start(bf16[2,8,8,48]{3,2,1,0:T(8,128)(2,1)S(1)} %bitcast.31), channel_id=1, source_target_pairs={{0,96},{32,0},{64,32},{96,64},{1,97},{33,1},{65,33},{97,65},{2,98}... | collective-permute-start | bytes 36872 | tf_op jit(solution)/shard_map/ppermute | solution.py:711
  172.3 4.8 %collective-permute-start.18 = (bf16[2,8,8,48]{3,2,1,0:T(8,128)(2,1)S(1)}, bf16[2,8,8,48]{3,2,1,0:T(8,128)(2,1)S(1)}, u32[]{:S(2)}, u32[]{:S(2)}) collective-permute-start(bf16[2,8,8,48]{3,2,1,0:T(8,128)(2,1)S(1)} %bitcast.30), channel_id=1, source_target_pairs={{0,32},{32,64},{64,96},{96,0},{1,33},{33,65},{65,97},{97,1},{2,34}... | collective-permute-start | bytes 36872 | tf_op jit(solution)/shard_map/ppermute | solution.py:711
  177.2 3.8 %collective-permute-start.20 = (bf16[4,2,8,48]{3,2,1,0:T(8,128)(2,1)S(1)}, bf16[4,2,8,48]{3,2,1,0:T(8,128)(2,1)S(1)}, u32[]{:S(2)}, u32[]{:S(2)}) collective-permute-start(bf16[4,2,8,48]{3,2,1,0:T(8,128)(2,1)S(1)} %get-tuple-element.56), channel_id=1, source_target_pairs={{0,8},{8,16},{16,24},{24,0},{1,9},{9,17},{17,25},{25,1},{2,10},{10... | collective-permute-start | bytes 18440 | tf_op jit(solution)/shard_map/ppermute | solution.py:711
  178.6 4.9 %collective-permute-start.21 = (bf16[4,2,8,48]{3,2,1,0:T(8,128)(2,1)S(1)}, bf16[4,2,8,48]{3,2,1,0:T(8,128)(2,1)S(1)}, u32[]{:S(2)}, u32[]{:S(2)}) collective-permute-start(bf16[4,2,8,48]{3,2,1,0:T(8,128)(2,1)S(1)} %get-tuple-element.57), channel_id=1, source_target_pairs={{0,24},{8,0},{16,8},{24,16},{1,25},{9,1},{17,9},{25,17},{2,26},{10... | collective-permute-start | bytes 18440 | tf_op jit(solution)/shard_map/ppermute | solution.py:711
  183.6 5.8 %collective-permute-start.22 = (bf16[4,4,2,48]{3,2,1,0:T(2,128)(2,1)S(1)}, bf16[4,4,2,48]{3,2,1,0:T(2,128)(2,1)S(1)}, u32[]{:S(2)}, u32[]{:S(2)}) collective-permute-start(bf16[4,4,2,48]{3,2,1,0:T(2,128)(2,1)S(1)} %get-tuple-element.60), channel_id=1, source_target_pairs={{0,1},{1,2},{2,3},{3,4},{4,5},{5,6},{6,7},{7,0},{8,9},{9,10},{10,1... | collective-permute-start | bytes 9224 | tf_op jit(solution)/shard_map/ppermute | solution.py:711
  183.7 5.8 %collective-permute-start.23 = (bf16[4,4,2,48]{3,2,1,0:T(2,128)(2,1)S(1)}, bf16[4,4,2,48]{3,2,1,0:T(2,128)(2,1)S(1)}, u32[]{:S(2)}, u32[]{:S(2)}) collective-permute-start(bf16[4,4,2,48]{3,2,1,0:T(2,128)(2,1)S(1)} %get-tuple-element.61), channel_id=1, source_target_pairs={{0,7},{1,0},{2,1},{3,2},{4,3},{5,4},{6,5},{7,6},{8,15},{9,8},{10,9... | collective-permute-start | bytes 9224 | tf_op jit(solution)/shard_map/ppermute | solution.py:711
